TPU v7x, 32 devices: a whole 2x2x4 slice. The times are simulated.
32 devices in a mesh: gx: 16 (over z, y, core), gy: 2 (over x).
Axes of the slice: x: 2, y: 2, z: 4, core: 2. Of those that a mesh axis runs over, the one named last changes fastest.
Arguments:
- source: float32 [64, 64, 256], P('gx', 'gy'), may hold values from -96 to 96
- region: int32 [64, 64, 256], P('gx', 'gy'), may hold values from 0 to 63
- permeability: float32 [64], replicated, may hold values from 0.1 to 10
- owners: int32 [16, 2], P('gx'), may hold values from 0 to 1
Outputs:
- pressure: float32 [64, 64, 256], P('gx', 'gy')
All inputs are finite; a program needn't handle non-finite values.
Results may differ from a plain program's by a relative error of at most 0.0001.
Values sent between devices are 32-bit elements; how exact they have to be, the bound alone decides.
A program may use at most 64 MiB of HBM per device.

v0:
```python
import functools

import jax
import jax.numpy as jnp
from jax import lax
from jax.experimental import pallas as pl
from jax.experimental.pallas import tpu as pltpu
from jax.sharding import PartitionSpec as P

POST_SWEEPS = 2
COARSE_SWEEPS = 6
RELAX_WEIGHT = 0.6
MASS_TERM = 0.1

MESH = pl.DeviceIdType.MESH
WIDE = 3
HALF = 4
COND, SOURCE, ITERATE = 0, 1, 2
WIDTHS = (3, 2, 2)
STEPS = ((-1, 0), (1, 0), (0, -1), (0, 1), (-1, -1), (1, -1), (-1, 1), (1, 1))


def kernel(
    n_gx, n_gy,
    owners_in, table_in, source_ref, region_ref, out_ref,
    owners_ref, table_ref, ext, packed, after, before, labels, weight, diag2, group, squeezed, whole_corr, spread, corr, corr_y, wide,
    send_sem, recv_sem, g_send, g_recv, in_sem, c_send, c_recv,
):
    nx, ny, nz = out_ref.shape
    cx, cy, cz = nx // 2, ny // 2, nz // 2
    first, last = WIDE, WIDE + nx
    gx, gy = lax.axis_index("gx"), lax.axis_index("gy")

    def exists(dx, dy):
        x, y = gx + dx, gy + dy
        return (x >= 0) & (x < n_gx) & (y >= 0) & (y < n_gy)

    load_source = pltpu.make_async_copy(
        source_ref, ext.at[SOURCE, pl.ds(first, nx), pl.ds(0, ny)], in_sem.at[0]
    )
    load_region = pltpu.make_async_copy(region_ref, labels, in_sem.at[1])
    load_table = pltpu.make_async_copy(table_in, table_ref, in_sem.at[2])
    load_owners = pltpu.make_async_copy(owners_in, owners_ref, in_sem.at[3])
    load_region.start()
    load_table.start()
    load_source.start()
    load_owners.start()

    barrier = pltpu.get_barrier_semaphore()
    count = jnp.int32(0)
    for dx, dy in STEPS:
        near = exists(dx, dy)

        @pl.when(near)
        def _():
            pl.semaphore_signal(
                barrier, inc=1, device_id=(gx + dx, gy + dy), device_id_type=MESH
            )

        count = count + near.astype(jnp.int32)
    for off in range(2 - n_gy - 1, n_gy):
        if abs(off) >= 2:
            near = exists(0, off)

            @pl.when(near)
            def _():
                pl.semaphore_signal(
                    barrier, inc=1, device_id=(gx, gy + off), device_id_type=MESH
                )

            count = count + near.astype(jnp.int32)

    def planes_in(dx, w):
        return {0: (first, nx), -1: (last, w), 1: (first - w, w)}[dx]

    def planes_out(dx, w):
        return {0: (first, nx), -1: (first, w), 1: (last - w, w)}[dx]

    def landing(kind, dx, dy, w):
        start, size = planes_in(dx, w)
        if dy == 0:
            return ext.at[kind, pl.ds(start, size), pl.ds(0, ny)]
        start, size = {0: (2, cx), -1: (2 + cx, (w + 1) // 2), 1: (2 - (w + 1) // 2, (w + 1) // 2)}[dx]
        return (after if dy < 0 else before).at[kind, pl.ds(start, size)]

    def remote(kind, which):
        dx, dy = STEPS[which]
        w = WIDTHS[kind]
        start, size = planes_out(dx, w)
        if dy == 0:
            source = ext.at[kind, pl.ds(start, size), pl.ds(0, ny)]
        else:
            tiles = (w + 1) // 2
            start, size = {0: (0, cx), -1: (0, tiles), 1: (cx - tiles, tiles)}[dx]
            source = packed.at[kind, max(dy, 0), pl.ds(start, size)]
        return pltpu.make_async_remote_copy(
            src_ref=source,
            dst_ref=landing(kind, dx, dy, w),
            send_sem=send_sem.at[kind, which],
            recv_sem=recv_sem.at[kind, which],
            device_id=(gx + dx, gy + dy),
            device_id_type=MESH,
        )

    def landing_corr(dx, dy):
        at = {0: pl.ds(1, cx), -1: pl.ds(cx + 1, 1), 1: pl.ds(0, 1)}[dx]
        return corr.at[at] if dy == 0 else corr_y.at[max(dy, 0), at]

    def remote_corr(which):
        dx, dy = STEPS[which]
        at = {0: pl.ds(1, cx), -1: pl.ds(1, 1), 1: pl.ds(cx, 1)}[dx]
        rows = {0: pl.ds(0, cy), -1: pl.ds(0, 8), 1: pl.ds(cy - 8, 8)}[dy]
        return pltpu.make_async_remote_copy(
            src_ref=corr.at[at, rows],
            dst_ref=landing_corr(dx, dy),
            send_sem=c_send.at[which],
            recv_sem=c_recv.at[which],
            device_id=(gx + dx, gy + dy),
            device_id_type=MESH,
        )

    def send(kind):
        for which, (dx, dy) in enumerate(STEPS):
            @pl.when(exists(dx, dy))
            def _():
                remote(kind, which).start()

    def receive(kind):
        for which, (dx, dy) in enumerate(STEPS):
            @pl.when(exists(-dx, -dy))
            def _():
                remote(kind, which).wait_recv()

    def finish(kind):
        for which, (dx, dy) in enumerate(STEPS):
            @pl.when(exists(dx, dy))
            def _():
                remote(kind, which).wait_send()

    for dx, dy in STEPS:
        @pl.when(jnp.logical_not(exists(-dx, -dy)))
        def _():
            for kind in range(3):
                ref = landing(kind, dx, dy, WIDTHS[kind])
                ref[...] = jnp.zeros(ref.shape, jnp.float32)
            ref = landing_corr(dx, dy)
            ref[...] = jnp.zeros(ref.shape, jnp.float32)

    row8 = lax.broadcasted_iota(jnp.int32, (8, nz), 0)

    def pack(kind):
        for s in range(cx):
            a, b = first + 2 * s, first + 2 * s + 1
            packed[kind, 0, s] = jnp.where(
                row8 < HALF, ext[kind, a, pl.ds(0, 8), :],
                pltpu.roll(ext[kind, b, pl.ds(0, 8), :], HALF, 0),
            )
            packed[kind, 1, s] = jnp.where(
                row8 < HALF, pltpu.roll(ext[kind, a, pl.ds(ny - 8, 8), :], HALF, 0),
                ext[kind, b, pl.ds(ny - 8, 8), :],
            )

    def join(kind):
        w = WIDTHS[kind]
        for i in range(first - w, last + w):
            s, odd = divmod(i - first + 4, 2)
            low, high = after[kind, s], before[kind, s]
            if odd:
                low = pltpu.roll(low, HALF, 0)
            else:
                high = pltpu.roll(high, HALF, 0)
            ext[kind, i, pl.ds(ny, 8), :] = jnp.where(row8 < HALF, low, high)

    load_table.wait()
    load_region.wait()
    pair = jnp.concatenate([table_ref[...], table_ref[...]], axis=1)
    table = jnp.broadcast_to(pair, (8, 128))
    for i in range(nx):
        for r in range(0, ny, 8):
            for c in range(0, nz, 128):
                spot = labels[i, pl.ds(r, 8), pl.ds(c, 128)]
                ext[COND, first + i, pl.ds(r, 8), pl.ds(c, 128)] = jnp.take_along_axis(
                    table, spot, axis=1
                )

    pack(COND)
    pl.semaphore_wait(barrier, count)
    send(COND)
    load_source.wait()
    pack(SOURCE)
    send(SOURCE)
    load_owners.wait()

    lane = lax.broadcasted_iota(jnp.int32, (1, nz), 1)
    z_low = jnp.where(lane == 0, 0.0, 0.5)
    z_high = jnp.where(lane == nz - 1, 0.0, 0.5)
    rows = ny + 8

    def blend(a, b, c, keep=rows):
        u = b + 0.5 * (a + c)
        u = u + 0.5 * (pltpu.roll(u, 1, 0) + pltpu.roll(u, rows - 1, 0))
        u = u[:keep]
        return u + z_low * pltpu.roll(u, 1, 1) + z_high * pltpu.roll(u, nz - 1, 1)

    lane128 = lax.broadcasted_iota(jnp.int32, (8, 128), 1)
    even = lax.rem(2 * lane128, jnp.int32(128))
    half_of = lane128 // 2

    def coarsen(pairs, kind):
        for i, pair_sum in enumerate(pairs):
            total = pair_sum + pltpu.roll(pair_sum, nz - 1, 1)
            for r in range(0, ny, 8):
                low = jnp.take_along_axis(total[r:r + 8, :128], even, axis=1)
                high = jnp.take_along_axis(total[r:r + 8, 128:], even, axis=1)
                squeezed[i, pl.ds(r, 8), :] = jnp.where(lane128 < 64, low, high)
            block = squeezed[i, pl.ds(0, cy, stride=2), :] + squeezed[i, pl.ds(1, cy, stride=2), :]
            group[kind, i, pl.ds(pl.multiple_of(gy * cy, 8), cy), :] = 0.125 * block

    def gather(kind, off):
        mine = group.at[kind, :, pl.ds(pl.multiple_of(gy * cy, 8), cy)]
        return pltpu.make_async_remote_copy(
            src_ref=mine,
            dst_ref=mine,
            send_sem=g_send.at[kind, off - 1],
            recv_sem=g_recv.at[kind, off - 1],
            device_id=(gx, lax.rem(gy + off, n_gy)),
            device_id_type=MESH,
        )

    def gather_in(kind, off):
        sender = lax.rem(gy + n_gy - off, n_gy)
        theirs = group.at[kind, :, pl.ds(pl.multiple_of(sender * cy, 8), cy)]
        return pltpu.make_async_remote_copy(
            src_ref=theirs,
            dst_ref=theirs,
            send_sem=g_send.at[kind, off - 1],
            recv_sem=g_recv.at[kind, off - 1],
            device_id=(gx, sender),
            device_id_type=MESH,
        )

    coarsen(
        [ext[COND, first + 2 * i, pl.ds(0, ny), :] + ext[COND, first + 2 * i + 1, pl.ds(0, ny), :]
         for i in range(cx)],
        0,
    )
    for off in range(1, n_gy):
        gather(0, off).start()

    receive(COND)
    join(COND)
    row = lax.broadcasted_iota(jnp.int32, (rows, 1), 0)
    y = gy * ny + jnp.where(row < ny + HALF, row, row - rows)
    in_y = jnp.where((y >= 0) & (y < n_gy * ny), RELAX_WEIGHT, 0.0)
    for i in range(first - 2, last + 2):
        cond = ext[COND, i]
        mixed = blend(ext[COND, i - 1], cond, ext[COND, i + 1])
        x = gx * nx + (i - first)
        in_x = jnp.where((x >= 0) & (x < n_gx * nx), 1.0, 0.0)
        weight[i] = (in_y * in_x) / (MASS_TERM + 6.0 * cond + mixed)
        diag2[i] = MASS_TERM + 8.0 * cond + mixed

    def defect(kind, i, values, flux, keep=rows):
        at = pl.ds(0, keep)
        lhs = ext[COND, i, at] * blend(values[i - 1], values[i], values[i + 1], keep)
        rhs = blend(flux[i - 1], flux[i], flux[i + 1], keep)
        return ext[SOURCE, i, at] - diag2[i, at] * values[i][:keep] + lhs + rhs

    receive(SOURCE)
    join(SOURCE)
    values, flux = {}, {}
    for i in range(first - 2, last + 2):
        values[i] = weight[i] * ext[SOURCE, i]
        flux[i] = ext[COND, i] * values[i]
    smooth = {}
    for i in range(first - 1, last + 1):
        smooth[i] = values[i] + weight[i] * defect(SOURCE, i, values, flux)
    flux = {i: ext[COND, i] * smooth[i] for i in smooth}
    pairs = []
    for i in range(cx):
        j = first + 2 * i
        pairs.append(
            defect(SOURCE, j, smooth, flux, ny) + defect(SOURCE, j + 1, smooth, flux, ny)
        )
    coarsen(pairs, 1)
    for off in range(1, n_gy):
        gather(1, off).start()
    for i in range(first, last):
        ext[ITERATE, i, pl.ds(0, ny), :] = smooth[i][:ny]
    pack(ITERATE)
    send(ITERATE)

    all_y = n_gy * cy
    crow = lax.broadcasted_iota(jnp.int32, (all_y, cz), 0)
    clane = lax.broadcasted_iota(jnp.int32, (all_y, cz), 1)
    owner = jnp.full((all_y, cz), owners_ref[0, 0], jnp.int32)
    for c in range(1, n_gy):
        owner = jnp.where(crow >= c * cy, owners_ref[0, c], owner)
    mask = jnp.where(owner == owners_ref[0, gy], 1.0, 0.0)
    y_low = jnp.where(crow == 0, 0.0, 0.5)
    y_high = jnp.where(crow == all_y - 1, 0.0, 0.5)
    cz_low = jnp.where(clane == 0, 0.0, 0.5)
    cz_high = jnp.where(clane == cz - 1, 0.0, 0.5)

    def coarse_blend(planes):
        mixed = []
        for i, u in enumerate(planes):
            if i > 0:
                u = u + 0.5 * planes[i - 1]
            if i + 1 < cx:
                u = u + 0.5 * planes[i + 1]
            u = u + y_low * pltpu.roll(u, 1, 0) + y_high * pltpu.roll(u, all_y - 1, 0)
            mixed.append(u + cz_low * pltpu.roll(u, 1, 1) + cz_high * pltpu.roll(u, cz - 1, 1))
        return mixed

    for off in range(1, n_gy):
        gather_in(0, off).wait_recv()
    cond_c = [mask * group[0, i] for i in range(cx)]
    mixed = coarse_blend(cond_c)
    diag_c = [MASS_TERM + 1.5 * k + 0.25 * b for k, b in zip(cond_c, mixed)]
    weight_c = [RELAX_WEIGHT * mask / d for d in diag_c]
    diag_sum = jnp.sum(functools.reduce(jnp.add, [mask * d for d in diag_c]), keepdims=True)

    for off in range(1, n_gy):
        gather_in(1, off).wait_recv()
    res_c = [mask * group[1, i] for i in range(cx)]

    def coarse_defect(e):
        straight = coarse_blend(e)
        carried = coarse_blend([k * v for k, v in zip(cond_c, e)])
        return [
            res_c[i] - (diag_c[i] + 0.5 * cond_c[i]) * e[i]
            + 0.25 * (cond_c[i] * straight[i] + carried[i])
            for i in range(cx)
        ]

    e = [w * r for w, r in zip(weight_c, res_c)]
    for _ in range(COARSE_SWEEPS - 1):
        d = coarse_defect(e)
        e = [e[i] + weight_c[i] * d[i] for i in range(cx)]
    d = coarse_defect(e)
    left = jnp.sum(functools.reduce(jnp.add, [mask * v for v in d]), keepdims=True)
    ratio = left / jnp.maximum(diag_sum, 1.0)
    for i in range(cx):
        whole_corr[i] = e[i] + mask * ratio
        corr[1 + i] = whole_corr[i, pl.ds(pl.multiple_of(gy * cy, 8), cy), :]
    for which, (dx, dy) in enumerate(STEPS):
        @pl.when(exists(dx, dy))
        def _():
            remote_corr(which).start()

    receive(ITERATE)
    join(ITERATE)
    for which, (dx, dy) in enumerate(STEPS):
        @pl.when(exists(-dx, -dy))
        def _():
            remote_corr(which).wait_recv()

    for i in range(cx + 2):
        mine = corr[i]
        spread[i, pl.ds(0, cy, stride=2), :] = mine
        spread[i, pl.ds(1, cy, stride=2), :] = mine
        for r in range(0, rows, 8):
            if r < ny:
                tile = spread[i, pl.ds(r, 8), :]
            else:
                tile = jnp.where(
                    lax.broadcasted_iota(jnp.int32, (8, cz), 0) < HALF,
                    jnp.broadcast_to(corr_y[0, i, pl.ds(0, 1), :], (8, cz)),
                    jnp.broadcast_to(corr_y[1, i, pl.ds(7, 1), :], (8, cz)),
                )
            for part in range(2):
                wide[i, pl.ds(r, 8), pl.ds(128 * part, 128)] = jnp.take_along_axis(
                    tile, half_of + 64 * part, axis=1
                )
    values = {
        i: ext[ITERATE, i] + wide[(i - first + 2) // 2] for i in range(first - 2, last + 2)
    }
    for sweep in range(POST_SWEEPS):
        reach = POST_SWEEPS - 1 - sweep
        keep = rows if reach else ny
        flux = {i: ext[COND, i] * values[i] for i in values}
        values = {
            i: values[i][:keep] + weight[i, pl.ds(0, keep)] * defect(ITERATE, i, values, flux, keep)
            for i in range(first - reach, last + reach)
        }
    for i in range(nx):
        out_ref[i] = values[first + i][:ny]

    for kind in range(3):
        finish(kind)
    for which, (dx, dy) in enumerate(STEPS):
        @pl.when(exists(dx, dy))
        def _():
            remote_corr(which).wait_send()

    for kind in range(2):
        for off in range(1, n_gy):
            gather(kind, off).wait_send()


def on_device(source, region, permeability, owners, *, n_gx, n_gy):
    nx, ny, nz = source.shape
    planes = nx + 2 * WIDE
    f32 = jnp.float32
    return pl.pallas_call(
        functools.partial(kernel, n_gx, n_gy),
        out_shape=jax.ShapeDtypeStruct(source.shape, f32),
        in_specs=[
            pl.BlockSpec(memory_space=pltpu.HBM),
            pl.BlockSpec(memory_space=pltpu.HBM),
            pl.BlockSpec(memory_space=pltpu.HBM),
            pl.BlockSpec(memory_space=pltpu.HBM),
        ],
        out_specs=pl.BlockSpec(memory_space=pltpu.VMEM),
        scratch_shapes=[
            pltpu.SMEM((1, n_gy), jnp.int32),
            pltpu.VMEM((1, permeability.shape[0]), f32),
            pltpu.VMEM((3, planes, ny + 8, nz), f32),
            pltpu.VMEM((3, 2, nx // 2, 8, nz), f32),
            pltpu.VMEM((3, nx // 2 + 4, 8, nz), f32),
            pltpu.VMEM((3, nx // 2 + 4, 8, nz), f32),
            pltpu.VMEM((nx, ny, nz), jnp.int32),
            pltpu.VMEM((planes, ny + 8, nz), f32),
            pltpu.VMEM((planes, ny + 8, nz), f32),
            pltpu.VMEM((2, nx // 2, n_gy * ny // 2, nz // 2), f32),
            pltpu.VMEM((nx // 2, ny, nz // 2), f32),
            pltpu.VMEM((nx // 2, n_gy * ny // 2, nz // 2), f32),
            pltpu.VMEM((nx // 2 + 2, ny, nz // 2), f32),
            pltpu.VMEM((nx // 2 + 2, ny // 2, nz // 2), f32),
            pltpu.VMEM((2, nx // 2 + 2, 8, nz // 2), f32),
            pltpu.VMEM((nx // 2 + 2, ny + 8, nz), f32),
            pltpu.SemaphoreType.DMA((3, 8)),
            pltpu.SemaphoreType.DMA((3, 8)),
            pltpu.SemaphoreType.DMA((2, n_gy - 1)),
            pltpu.SemaphoreType.DMA((2, n_gy - 1)),
            pltpu.SemaphoreType.DMA((4,)),
            pltpu.SemaphoreType.DMA((8,)),
            pltpu.SemaphoreType.DMA((8,)),
        ],
        compiler_params=pltpu.CompilerParams(
            collective_id=0, has_side_effects=True, vmem_limit_bytes=56328192
        ),
    )(owners, permeability[None, :], source, region)


def solution(mesh):
    placed = (P("gx", "gy", None), P("gx", "gy", None), P(), P("gx", None))
    body = functools.partial(on_device, n_gx=mesh.shape["gx"], n_gy=mesh.shape["gy"])
    return jax.shard_map(
        body, mesh=mesh, in_specs=placed, out_specs=P("gx", "gy", None), check_vma=False
    )
```

profile of v0, /device:TPU:1, one launch (start us, length us, event | category | flops | bytes accessed | tf_op | source)
XLA Modules:
  0.0 19.4 jit_solution(18432627635847782558)
XLA Ops:
  0.0 0.0 copy-start
  0.0 0.0 copy-start.1
  0.0 0.7 %copy-done = s32[1,2]{1,0:T(1,128)S(1)} copy-done((s32[1,2]{1,0:T(1,128)S(1)}, s32[1,2]{1,0:T(1,128)}, u32[]{:S(2)}) %copy-start) | copy-done | bytes 32
  0.7 0.0 copy-done.1
  0.7 18.0 %shard_map.46 = f32[4,32,256]{2,1,0:T(8,128)S(1)} custom-call(s32[1,2]{1,0:T(1,128)S(1)} %copy-done, f32[1,64]{1,0:T(1,128)S(1)} %bitcast.1, f32[4,32,256]{2,1,0:T(8,128)} %source_ref.1, s32[4,32,256]{2,1,0:T(8,128)} %region_ref.1), custom_call_target="tpu_custom_call" | custom-call | tf_op jit(solution)/shard_map/pallas_call | solution.py:406
  18.7 0.7 %copy.6 = f32[4,32,256]{2,1,0:T(8,128)} copy(f32[4,32,256]{2,1,0:T(8,128)S(1)} %shard_map.46) | data formatting | bytes 262144
Async XLA Ops:
  0.0 0.7 %copy-start = (s32[1,2]{1,0:T(1,128)S(1)}, s32[1,2]{1,0:T(1,128)}, u32[]{:S(2)}) copy-start(s32[1,2]{1,0:T(1,128)} %owners_in.1) | copy-start | bytes 28
  0.0 0.7 %copy-start.1 = (f32[64]{0:T(128)S(1)}, f32[64]{0:T(128)}, u32[]{:S(2)}) copy-start(f32[64]{0:T(128)} %param.6) | copy-start | bytes 772
where the time goes:
time: 19.5 us; the launch traced here: 19.4 us
  Pallas kernels  18 us (92%)
  local copies, waits for them, and re-layouts  1.33 us (7%)
    pallas_call x1, Pallas kernels, on_device(): pl.pallas_call(functools.partial(kernel, n_gx, n_gy), out_shape=jax.Shape...  18 us
    unnamed x5, local copies, waits for them, and re-layouts  1.33 us

commit v1 on v0

v1 whole, which is shorter than its diff:
```python
import functools

import jax
import jax.numpy as jnp
from jax import lax
from jax.experimental import pallas as pl
from jax.experimental.pallas import tpu as pltpu
from jax.sharding import PartitionSpec as P

POST_SWEEPS = 2
COARSE_SWEEPS = 6
RELAX_WEIGHT = 0.6
MASS_TERM = 0.1

MESH = pl.DeviceIdType.MESH
WIDE = 3
HALF = 4
REGION, SOURCE, ITERATE = 0, 1, 2
WIDTHS = (3, 2, 2)
STEPS = ((-1, -1), (1, -1), (-1, 1), (1, 1), (0, -1), (0, 1), (-1, 0), (1, 0))


def kernel(
    n_gx, n_gy,
    owners_in, table_in, source_ref, region_ref, out_ref,
    owners_ref, table_ref, labels, source, iterate, cond, weight, diag2, group, holders, squeezed, whole_corr, spread, wide,
    send_sem, recv_sem, g_send, g_recv, h_send, h_recv, in_sem,
):
    nx, ny, nz = out_ref.shape
    cx, cy, cz = nx // 2, ny // 2, nz // 2
    first, last = WIDE, WIDE + nx
    gx, gy = lax.axis_index("gx"), lax.axis_index("gy")
    fields = (labels, source, iterate)

    def exists(dx, dy):
        x, y = gx + dx, gy + dy
        return (x >= 0) & (x < n_gx) & (y >= 0) & (y < n_gy)

    near_slabs = [
        (dx, off) for dx in (-1, 1, 0) for off in reversed(range(n_gy)) if (dx, off) != (0, 0)
    ]

    barrier = pltpu.get_barrier_semaphore()
    count = jnp.int32(0)
    for dx, off in near_slabs:
        near = exists(dx, 0)

        @pl.when(near)
        def _():
            pl.semaphore_signal(
                barrier, inc=1, device_id=(gx + dx, lax.rem(gy + off, n_gy)), device_id_type=MESH
            )

        count = count + near.astype(jnp.int32)

    load_source = pltpu.make_async_copy(
        source_ref, source.at[pl.ds(first, nx), pl.ds(0, ny)], in_sem.at[0]
    )
    load_region = pltpu.make_async_copy(
        region_ref, labels.at[pl.ds(first, nx), pl.ds(0, ny)], in_sem.at[1]
    )
    load_table = pltpu.make_async_copy(table_in, table_ref, in_sem.at[2])
    load_owners = pltpu.make_async_copy(owners_in, owners_ref, in_sem.at[3])
    load_region.start()
    load_table.start()
    load_source.start()
    load_owners.start()

    def landing(kind, dx, dy):
        w = WIDTHS[kind]
        start, size = {0: (first, nx), -1: (last, w), 1: (first - w, w)}[dx]
        row, high = {0: (0, ny), -1: (ny, HALF), 1: (ny + HALF, HALF)}[dy]
        return fields[kind].at[pl.ds(start, size), pl.ds(row, high)]

    def remote(kind, which):
        dx, dy = STEPS[which]
        w = WIDTHS[kind]
        base = first if kind == ITERATE else 0
        start, size = {0: (0, nx), -1: (0, w), 1: (nx - w, w)}[dx]
        row, high = {0: (0, ny), -1: (0, HALF), 1: (ny - HALF, HALF)}[dy]
        origin = (region_ref, source_ref, iterate)[kind]
        return pltpu.make_async_remote_copy(
            src_ref=origin.at[pl.ds(base + start, size), pl.ds(row, high)],
            dst_ref=landing(kind, dx, dy),
            send_sem=send_sem.at[kind, which],
            recv_sem=recv_sem.at[kind, which],
            device_id=(gx + dx, gy + dy),
            device_id_type=MESH,
        )

    def send(kind):
        for which, (dx, dy) in enumerate(STEPS):
            @pl.when(exists(dx, dy))
            def _():
                remote(kind, which).start()

    def receive(kind, inner):
        for which, (dx, dy) in enumerate(STEPS):
            if (dx == 0) == inner:
                @pl.when(exists(-dx, -dy))
                def _():
                    remote(kind, which).wait_recv()

    def finish(kind):
        for which, (dx, dy) in enumerate(STEPS):
            @pl.when(exists(dx, dy))
            def _():
                remote(kind, which).wait_send()

    def gather(kind, dx, off):
        at = pl.ds(pl.multiple_of(gy * cy, 8), cy)
        return pltpu.make_async_remote_copy(
            src_ref=group.at[kind, 1, :, at],
            dst_ref=group.at[kind, 1 - dx, :, at],
            send_sem=g_send.at[kind, dx + 1, off],
            recv_sem=g_recv.at[kind, dx + 1, off],
            device_id=(gx + dx, lax.rem(gy + off, n_gy)),
            device_id_type=MESH,
        )

    def gather_in(kind, dx, off):
        sender = lax.rem(gy + n_gy - off, n_gy)
        theirs = group.at[kind, 1 - dx, :, pl.ds(pl.multiple_of(sender * cy, 8), cy)]
        return pltpu.make_async_remote_copy(
            src_ref=theirs,
            dst_ref=theirs,
            send_sem=g_send.at[kind, dx + 1, off],
            recv_sem=g_recv.at[kind, dx + 1, off],
            device_id=(gx - dx, sender),
            device_id_type=MESH,
        )

    def tell(dx):
        return pltpu.make_async_remote_copy(
            src_ref=holders.at[1],
            dst_ref=holders.at[1 - dx],
            send_sem=h_send.at[(dx + 1) // 2],
            recv_sem=h_recv.at[(dx + 1) // 2],
            device_id=(gx + dx, gy),
            device_id_type=MESH,
        )

    def gather_start(kind):
        for dx, off in near_slabs:
            @pl.when(exists(dx, 0))
            def _():
                gather(kind, dx, off).start()

    def gather_wait(kind):
        for dx, off in near_slabs:
            @pl.when(exists(-dx, 0))
            def _():
                gather_in(kind, dx, off).wait_recv()

    for dx, dy in STEPS:
        @pl.when(jnp.logical_not(exists(-dx, -dy)))
        def _():
            ref = landing(REGION, dx, dy)
            ref[...] = jnp.full(ref.shape, table_ref.shape[1], jnp.int32)
            for kind in (SOURCE, ITERATE):
                ref = landing(kind, dx, dy)
                ref[...] = jnp.zeros(ref.shape, jnp.float32)
    for dx in (-1, 1):
        @pl.when(jnp.logical_not(exists(-dx, 0)))
        def _():
            for kind in range(2):
                ref = group.at[kind, 1 - dx]
                ref[...] = jnp.zeros(ref.shape, jnp.float32)
            ref = holders.at[1 - dx]
            ref[...] = jnp.zeros(ref.shape, jnp.float32)

    with jax.named_scope("wait_neighbours"):
        pl.semaphore_wait(barrier, count)
    send(REGION)
    send(SOURCE)

    load_table.wait()
    with jax.named_scope("wait_own_region"):
        load_region.wait()
    regions = table_ref.shape[1]
    pair = jnp.concatenate([table_ref[...], jnp.zeros((1, 128 - regions), jnp.float32)], axis=1)
    table = jnp.broadcast_to(pair, (8, 128))

    def look_up(planes, tiles):
        for i in planes:
            for r in tiles:
                for c in range(0, nz, 128):
                    spot = labels[i, pl.ds(r, 8), pl.ds(c, 128)]
                    cond[i, pl.ds(r, 8), pl.ds(c, 128)] = jnp.take_along_axis(table, spot, axis=1)

    look_up(range(first, last), range(0, ny, 8))

    lane = lax.broadcasted_iota(jnp.int32, (1, nz), 1)
    z_low = jnp.where(lane == 0, 0.0, 0.5)
    z_high = jnp.where(lane == nz - 1, 0.0, 0.5)
    rows = ny + 8

    def blend(a, b, c, keep=rows):
        u = b + 0.5 * (a + c)
        u = u + 0.5 * (pltpu.roll(u, 1, 0) + pltpu.roll(u, rows - 1, 0))
        u = u[:keep]
        return u + z_low * pltpu.roll(u, 1, 1) + z_high * pltpu.roll(u, nz - 1, 1)

    lane128 = lax.broadcasted_iota(jnp.int32, (8, 128), 1)
    even = lax.rem(2 * lane128, jnp.int32(128))
    half_of = lane128 // 2

    def coarsen(pairs, kind):
        for i, pair_sum in enumerate(pairs):
            total = pair_sum + pltpu.roll(pair_sum, nz - 1, 1)
            for r in range(0, ny, 8):
                low = jnp.take_along_axis(total[r:r + 8, :128], even, axis=1)
                high = jnp.take_along_axis(total[r:r + 8, 128:], even, axis=1)
                squeezed[i, pl.ds(r, 8), :] = jnp.where(lane128 < 64, low, high)
            block = squeezed[i, pl.ds(0, cy, stride=2), :] + squeezed[i, pl.ds(1, cy, stride=2), :]
            group[kind, 1, i, pl.ds(pl.multiple_of(gy * cy, 8), cy), :] = 0.125 * block

    coarsen(
        [cond[first + 2 * i, pl.ds(0, ny), :] + cond[first + 2 * i + 1, pl.ds(0, ny), :]
         for i in range(cx)],
        0,
    )
    load_owners.wait()
    for c in range(n_gy):
        holders[1, c] = jnp.full((8, cz), owners_ref[0, c].astype(jnp.float32))

    row = lax.broadcasted_iota(jnp.int32, (rows, 1), 0)
    y = gy * ny + jnp.where(row < ny + HALF, row, row - rows)
    in_y = jnp.where((y >= 0) & (y < n_gy * ny), RELAX_WEIGHT, 0.0)

    def weigh(planes):
        for i in planes:
            mine = cond[i]
            mixed = blend(cond[i - 1], mine, cond[i + 1])
            x = gx * nx + (i - first)
            in_x = jnp.where((x >= 0) & (x < n_gx * nx), 1.0, 0.0)
            weight[i] = (in_y * in_x) / (MASS_TERM + 6.0 * mine + mixed)
            diag2[i] = MASS_TERM + 8.0 * mine + mixed

    with jax.named_scope("wait_region_rows"):
        receive(REGION, True)
    look_up(range(first, last), (ny,))
    weigh(range(first + 1, last - 1))
    with jax.named_scope("wait_region_planes"):
        receive(REGION, False)
    edges = [*range(first - WIDE, first), *range(last, last + WIDE)]
    look_up(edges, range(0, rows, 8))
    weigh([first - 2, first - 1, first, last - 1, last, last + 1])
    with jax.named_scope("start_coarse_cond"):
        gather_start(0)
    for dx in (-1, 1):
        @pl.when(exists(dx, 0))
        def _():
            tell(dx).start()

    def defect(i, values, flux, keep=rows):
        at = pl.ds(0, keep)
        lhs = cond[i, at] * blend(values[i - 1], values[i], values[i + 1], keep)
        rhs = blend(flux[i - 1], flux[i], flux[i + 1], keep)
        return source[i, at] - diag2[i, at] * values[i][:keep] + lhs + rhs

    load_source.wait()
    with jax.named_scope("wait_source_rows"):
        receive(SOURCE, True)
    with jax.named_scope("wait_source_planes"):
        receive(SOURCE, False)
    values, flux = {}, {}
    for i in range(first - 2, last + 2):
        values[i] = weight[i] * source[i]
        flux[i] = cond[i] * values[i]
    smooth = {}
    for i in range(first - 1, last + 1):
        smooth[i] = values[i] + weight[i] * defect(i, values, flux)
    flux = {i: cond[i] * smooth[i] for i in smooth}
    pairs = []
    for i in range(cx):
        j = first + 2 * i
        pairs.append(defect(j, smooth, flux, ny) + defect(j + 1, smooth, flux, ny))
    coarsen(pairs, 1)
    with jax.named_scope("start_coarse_res"):
        gather_start(1)
    for i in range(first, last):
        iterate[i, pl.ds(0, ny), :] = smooth[i][:ny]
    send(ITERATE)

    all_y = n_gy * cy
    crow = lax.broadcasted_iota(jnp.int32, (all_y, cz), 0)
    clane = lax.broadcasted_iota(jnp.int32, (1, cz), 1)
    cz_low = jnp.where(clane == 0, 0.0, 0.5)
    cz_high = jnp.where(clane == cz - 1, 0.0, 0.5)

    def coarse_blend(planes, y_low, y_high):
        mixed = []
        for i, u in enumerate(planes):
            near = [planes[j] for j in (i - 1, i + 1) if 0 <= j < cx]
            u = u + 0.5 * functools.reduce(jnp.add, near) if near else u
            u = u + y_low * pltpu.roll(u, 1, 0) + y_high * pltpu.roll(u, all_y - 1, 0)
            mixed.append(u + cz_low * pltpu.roll(u, 1, 1) + cz_high * pltpu.roll(u, cz - 1, 1))
        return mixed

    def total(planes, c):
        whole = functools.reduce(jnp.add, [v[c * cy:(c + 1) * cy] for v in planes])
        return jnp.sum(whole, keepdims=True)

    with jax.named_scope("wait_holders"):
        for dx in (-1, 1):
            @pl.when(exists(-dx, 0))
            def _():
                tell(dx).wait_recv()
    with jax.named_scope("wait_coarse_cond"):
        gather_wait(0)
    slabs = []
    for g in range(3):
        held = [holders[g, c, pl.ds(0, 1), :] for c in range(n_gy)]
        same = lambda a, b: jnp.where(held[a] == held[b], 1.0, 0.0)
        y_low = jnp.where(crow == 0, 0.0, 0.5)
        y_high = jnp.where(crow == all_y - 1, 0.0, 0.5)
        for c in range(1, n_gy):
            tied = 0.5 * same(c - 1, c)
            y_low = jnp.where(crow == c * cy, tied, y_low)
            y_high = jnp.where(crow == c * cy - 1, tied, y_high)
        k = [group[0, g, i] for i in range(cx)]
        mixed = coarse_blend(k, y_low, y_high)
        diag = [MASS_TERM + 1.5 * a + 0.25 * b for a, b in zip(k, mixed)]
        step = [RELAX_WEIGHT / d for d in diag]
        ones = coarse_blend([jnp.ones((all_y, cz), jnp.float32)] * cx, y_low, y_high)
        slabs.append(dict(
            y_low=y_low, y_high=y_high, k=k, step=step,
            keep=[1.0 - s * (d + 0.5 * a) for s, d, a in zip(step, diag, k)],
            mine=[0.25 * s * a for s, a in zip(step, k)],
            theirs=[0.25 * s for s in step],
            drain=[MASS_TERM + 0.25 * a * (8.0 - b) for a, b in zip(k, ones)],
            same=[[same(a, b)[:, :1] for b in range(n_gy)] for a in range(n_gy)],
            diag_sum=[total(diag, c) for c in range(n_gy)],
        ))

    with jax.named_scope("wait_coarse_res"):
        gather_wait(1)
    e = []
    for g, s in enumerate(slabs):
        s["res"] = [group[1, g, i] for i in range(cx)]
        s["start"] = [a * b for a, b in zip(s["step"], s["res"])]
        e.append(s["start"])
    for _ in range(COARSE_SWEEPS - 1):
        for g, s in enumerate(slabs):
            straight = coarse_blend(e[g], s["y_low"], s["y_high"])
            carried = coarse_blend([a * v for a, v in zip(s["k"], e[g])], s["y_low"], s["y_high"])
            e[g] = [
                s["start"][i] + s["keep"][i] * e[g][i]
                + (s["mine"][i] * straight[i] + s["theirs"][i] * carried[i])
                for i in range(cx)
            ]
    keep_planes = ((0, cx - 1), *[(1, i) for i in range(cx)], (2, 0))
    ratios = []
    for g, s in enumerate(slabs):
        left = [r - d * v for r, d, v in zip(s["res"], s["drain"], e[g])]
        left = [total(left, c) for c in range(n_gy)]
        shares = []
        for c in range(n_gy):
            num = functools.reduce(jnp.add, [s["same"][c][b] * left[b] for b in range(n_gy)])
            den = functools.reduce(jnp.add, [s["same"][c][b] * s["diag_sum"][b] for b in range(n_gy)])
            shares.append(num / jnp.maximum(den, 1.0))
        ratios.append(shares)
    for slot, (g, i) in enumerate(keep_planes):
        whole_corr[slot, pl.ds(0, 8), :] = jnp.zeros((8, cz), jnp.float32)
        whole_corr[slot, pl.ds(8 + all_y, 8), :] = jnp.zeros((8, cz), jnp.float32)
        for c in range(n_gy):
            whole_corr[slot, pl.ds(8 + c * cy, cy), :] = e[g][i][c * cy:(c + 1) * cy] + ratios[g][c]

    sub = lax.broadcasted_iota(jnp.int32, (8, cz), 0)
    for i in range(cx + 2):
        mine = whole_corr[i, pl.ds(pl.multiple_of(8 + gy * cy, 8), cy), :]
        below = whole_corr[i, pl.ds(pl.multiple_of(gy * cy, 8), 8), :]
        above = whole_corr[i, pl.ds(pl.multiple_of(8 + gy * cy + cy, 8), 8), :]
        spread[i, pl.ds(0, cy, stride=2), :] = mine
        spread[i, pl.ds(1, cy, stride=2), :] = mine
        for r in range(0, rows, 8):
            if r < ny:
                tile = spread[i, pl.ds(r, 8), :]
            else:
                tile = jnp.where(
                    sub < HALF,
                    jnp.broadcast_to(above[:1], (8, cz)),
                    jnp.broadcast_to(below[7:], (8, cz)),
                )
            for part in range(2):
                wide[i, pl.ds(r, 8), pl.ds(128 * part, 128)] = jnp.take_along_axis(
                    tile, half_of + 64 * part, axis=1
                )
    with jax.named_scope("wait_iterate_rows"):
        receive(ITERATE, True)
    with jax.named_scope("wait_iterate_planes"):
        receive(ITERATE, False)
    values = {
        i: iterate[i] + wide[(i - first + 2) // 2] for i in range(first - 2, last + 2)
    }
    for sweep in range(POST_SWEEPS):
        reach = POST_SWEEPS - 1 - sweep
        keep = rows if reach else ny
        flux = {i: cond[i] * values[i] for i in values}
        values = {
            i: values[i][:keep] + weight[i, pl.ds(0, keep)] * defect(i, values, flux, keep)
            for i in range(first - reach, last + reach)
        }
    for i in range(nx):
        out_ref[i] = values[first + i][:ny]

    with jax.named_scope("wait_sends"):
        for kind in range(3):
            finish(kind)
        for dx in (-1, 1):
            @pl.when(exists(dx, 0))
            def _():
                tell(dx).wait_send()
        for kind in range(2):
            for dx, off in near_slabs:
                @pl.when(exists(dx, 0))
                def _():
                    gather(kind, dx, off).wait_send()


def on_device(source, region, permeability, owners, *, n_gx, n_gy):
    nx, ny, nz = source.shape
    planes = nx + 2 * WIDE
    cx, all_y, cz = nx // 2, n_gy * ny // 2, nz // 2
    f32 = jnp.float32
    return pl.pallas_call(
        functools.partial(kernel, n_gx, n_gy),
        out_shape=jax.ShapeDtypeStruct(source.shape, f32),
        in_specs=[pl.BlockSpec(memory_space=pltpu.HBM)] * 4,
        out_specs=pl.BlockSpec(memory_space=pltpu.VMEM),
        scratch_shapes=[
            pltpu.SMEM((1, n_gy), jnp.int32),
            pltpu.VMEM((1, permeability.shape[0]), f32),
            pltpu.VMEM((planes, ny + 8, nz), jnp.int32),
            pltpu.VMEM((planes, ny + 8, nz), f32),
            pltpu.VMEM((planes, ny + 8, nz), f32),
            pltpu.VMEM((planes, ny + 8, nz), f32),
            pltpu.VMEM((planes, ny + 8, nz), f32),
            pltpu.VMEM((planes, ny + 8, nz), f32),
            pltpu.VMEM((2, 3, cx, all_y, cz), f32),
            pltpu.VMEM((3, n_gy, 8, cz), f32),
            pltpu.VMEM((cx, ny, cz), f32),
            pltpu.VMEM((cx + 2, all_y + 16, cz), f32),
            pltpu.VMEM((cx + 2, ny, cz), f32),
            pltpu.VMEM((cx + 2, ny + 8, nz), f32),
            pltpu.SemaphoreType.DMA((3, 8)),
            pltpu.SemaphoreType.DMA((3, 8)),
            pltpu.SemaphoreType.DMA((2, 3, n_gy)),
            pltpu.SemaphoreType.DMA((2, 3, n_gy)),
            pltpu.SemaphoreType.DMA((2,)),
            pltpu.SemaphoreType.DMA((2,)),
            pltpu.SemaphoreType.DMA((4,)),
        ],
        compiler_params=pltpu.CompilerParams(
            collective_id=0, has_side_effects=True, vmem_limit_bytes=56328192
        ),
    )(*[
        pltpu.with_memory_space_constraint(a, pltpu.HBM)
        for a in (owners, permeability[None, :], source, region)
    ])


def solution(mesh):
    placed = (P("gx", "gy", None), P("gx", "gy", None), P(), P("gx", None))
    body = functools.partial(on_device, n_gx=mesh.shape["gx"], n_gy=mesh.shape["gy"])
    return jax.shard_map(
        body, mesh=mesh, in_specs=placed, out_specs=P("gx", "gy", None), check_vma=False
    )
```

time: 19.5 us -> 16.3 us (0.84)
  Pallas kernels: 18 us -> 15.5 us
  local copies, waits for them, and re-layouts: 1.33 us -> 0.66 us
    pallas_call x1, Pallas kernels: 18 us -> 15.5 us  [on_device(): pl.pallas_call(functools.partial(kernel, n_gx, n_gy), out_shape=jax.Shape...]
    unnamed x5 -> x1, local copies, waits for them, and re-layouts: 1.33 us -> 0.66 us
where the time goes in v1:
time: 16.3 us; the launch traced here: 16.1 us
  Pallas kernels  15.5 us (95%)
  local copies, waits for them, and re-layouts  0.66 us (4%)
    pallas_call x1, Pallas kernels, on_device(): pl.pallas_call(functools.partial(kernel, n_gx, n_gy), out_shape=jax.Shape...  15.5 us
    unnamed x1, local copies, waits for them, and re-layouts  0.66 us

profile of v1, /device:TPU:1, one launch (start us, length us, event | category | flops | bytes accessed | tf_op | source)
XLA Modules:
  0.0 16.1 jit_solution(17088987351830694951)
XLA Ops:
  0.0 15.5 %shard_map.46 = f32[4,32,256]{2,1,0:T(8,128)S(1)} custom-call(s32[1,2]{1,0:T(1,128)} %owners_in.1, f32[1,64]{1,0:T(1,128)} %bitcast.1, f32[4,32,256]{2,1,0:T(8,128)} %source_ref.1, s32[4,32,256]{2,1,0:T(8,128)} %region_ref.1), custom_call_target="tpu_custom_call" | custom-call | tf_op jit(solution)/shard_map/pallas_call | solution.py:427
  15.5 0.7 %copy.6 = f32[4,32,256]{2,1,0:T(8,128)} copy(f32[4,32,256]{2,1,0:T(8,128)S(1)} %shard_map.46) | data formatting | bytes 262144

commit v2 on v1

--- a/solution.py
+++ b/solution.py
@@ -23,14 +23,19 @@
 def kernel(
     n_gx, n_gy,
     owners_in, table_in, source_ref, region_ref, out_ref,
-    owners_ref, table_ref, labels, source, iterate, cond, weight, diag2, group, holders, squeezed, whole_corr, spread, wide,
-    send_sem, recv_sem, g_send, g_recv, h_send, h_recv, in_sem,
+    owners_ref, table_ref, labels, store, group, holders, squeezed, whole_corr, spread, wide,
+    send_sem, recv_sem, in_sem,
 ):
     nx, ny, nz = out_ref.shape
     cx, cy, cz = nx // 2, ny // 2, nz // 2
     first, last = WIDE, WIDE + nx
     gx, gy = lax.axis_index("gx"), lax.axis_index("gy")
+    planes = nx + 2 * WIDE
+    source, iterate, cond, weight, diag2 = (
+        store.at[pl.ds(k * planes, planes)] for k in range(5)
+    )
     fields = (labels, source, iterate)
+    all_y = n_gy * cy
 
     def exists(dx, dy):
         x, y = gx + dx, gy + dy
@@ -82,8 +87,8 @@
         return pltpu.make_async_remote_copy(
             src_ref=origin.at[pl.ds(base + start, size), pl.ds(row, high)],
             dst_ref=landing(kind, dx, dy),
-            send_sem=send_sem.at[kind, which],
-            recv_sem=recv_sem.at[kind, which],
+            send_sem=send_sem.at[abs(dx)],
+            recv_sem=recv_sem.at[2 * kind + abs(dx)],
             device_id=(gx + dx, gy + dy),
             device_id_type=MESH,
         )
@@ -94,39 +99,45 @@
             def _():
                 remote(kind, which).start()
 
+    def by_neighbours(act):
+        for a in (1, 2):
+            for b in (1, 2) if n_gy > 2 else (1,):
+                xs = exists(-1, 0).astype(jnp.int32) + exists(1, 0).astype(jnp.int32)
+                ys = exists(0, -1).astype(jnp.int32) + exists(0, 1).astype(jnp.int32)
+
+                @pl.when((xs == a) & (ys == b))
+                def _():
+                    act(a, b)
+
+    def wait(ref, sem):
+        pltpu.make_async_copy(ref, ref, sem).wait()
+
+    def of_rows(n):
+        high = next(r for r in (40, 32, 24, 16, 8, HALF) if n % r == 0 and r <= store.shape[1])
+        return store.at[pl.ds(0, n // high), pl.ds(0, high)]
+
     def receive(kind, inner):
-        for which, (dx, dy) in enumerate(STEPS):
-            if (dx == 0) == inner:
-                @pl.when(exists(-dx, -dy))
-                def _():
-                    remote(kind, which).wait_recv()
-
-    def finish(kind):
-        for which, (dx, dy) in enumerate(STEPS):
-            @pl.when(exists(dx, dy))
-            def _():
-                remote(kind, which).wait_send()
+        def act(a, b):
+            n = nx * b * HALF if inner else a * WIDTHS[kind] * (ny + b * HALF)
+            wait(of_rows(n), recv_sem.at[2 * kind + 1 - inner])
+
+        by_neighbours(act)
+
+    def finish(a, b):
+        wait(of_rows(3 * nx * b * HALF), send_sem.at[0])
+        wait(of_rows(sum(WIDTHS) * a * (ny + b * HALF)), send_sem.at[1])
+        wait(group.at[:, :, pl.ds(0, (a * n_gy + n_gy - 1) * cy)], send_sem.at[2])
+        wait(holders.at[pl.ds(0, a)], send_sem.at[3])
 
     def gather(kind, dx, off):
-        at = pl.ds(pl.multiple_of(gy * cy, 8), cy)
+        at = pl.ds(pl.multiple_of(all_y + gy * cy, 8), cy)
+        to = pl.ds(pl.multiple_of((1 - dx) * all_y + gy * cy, 8), cy)
         return pltpu.make_async_remote_copy(
-            src_ref=group.at[kind, 1, :, at],
-            dst_ref=group.at[kind, 1 - dx, :, at],
-            send_sem=g_send.at[kind, dx + 1, off],
-            recv_sem=g_recv.at[kind, dx + 1, off],
+            src_ref=group.at[kind, :, at],
+            dst_ref=group.at[kind, :, to],
+            send_sem=send_sem.at[2],
+            recv_sem=recv_sem.at[6 + kind],
             device_id=(gx + dx, lax.rem(gy + off, n_gy)),
-            device_id_type=MESH,
-        )
-
-    def gather_in(kind, dx, off):
-        sender = lax.rem(gy + n_gy - off, n_gy)
-        theirs = group.at[kind, 1 - dx, :, pl.ds(pl.multiple_of(sender * cy, 8), cy)]
-        return pltpu.make_async_remote_copy(
-            src_ref=theirs,
-            dst_ref=theirs,
-            send_sem=g_send.at[kind, dx + 1, off],
-            recv_sem=g_recv.at[kind, dx + 1, off],
-            device_id=(gx - dx, sender),
             device_id_type=MESH,
         )
 
@@ -134,8 +145,8 @@
         return pltpu.make_async_remote_copy(
             src_ref=holders.at[1],
             dst_ref=holders.at[1 - dx],
-            send_sem=h_send.at[(dx + 1) // 2],
-            recv_sem=h_recv.at[(dx + 1) // 2],
+            send_sem=send_sem.at[3],
+            recv_sem=recv_sem.at[8],
             device_id=(gx + dx, gy),
             device_id_type=MESH,
         )
@@ -147,10 +158,9 @@
                 gather(kind, dx, off).start()
 
     def gather_wait(kind):
-        for dx, off in near_slabs:
-            @pl.when(exists(-dx, 0))
-            def _():
-                gather_in(kind, dx, off).wait_recv()
+        by_neighbours(lambda a, b: wait(
+            group.at[kind, :, pl.ds(0, (a * n_gy + n_gy - 1) * cy)], recv_sem.at[6 + kind]
+        ))
 
     for dx, dy in STEPS:
         @pl.when(jnp.logical_not(exists(-dx, -dy)))
@@ -164,7 +174,7 @@
         @pl.when(jnp.logical_not(exists(-dx, 0)))
         def _():
             for kind in range(2):
-                ref = group.at[kind, 1 - dx]
+                ref = group.at[kind, :, pl.ds((1 - dx) * all_y, all_y)]
                 ref[...] = jnp.zeros(ref.shape, jnp.float32)
             ref = holders.at[1 - dx]
             ref[...] = jnp.zeros(ref.shape, jnp.float32)
@@ -173,6 +183,17 @@
         pl.semaphore_wait(barrier, count)
     send(REGION)
     send(SOURCE)
+
+    load_owners.wait()
+    eight = lax.broadcasted_iota(jnp.int32, (8, cz), 0)
+    held = jnp.zeros((8, cz), jnp.float32)
+    for c in range(n_gy):
+        held = jnp.where(eight == c, owners_ref[0, c].astype(jnp.float32), held)
+    holders[1] = held
+    for dx in (-1, 1):
+        @pl.when(exists(dx, 0))
+        def _():
+            tell(dx).start()
 
     load_table.wait()
     with jax.named_scope("wait_own_region"):
@@ -213,16 +234,13 @@
                 high = jnp.take_along_axis(total[r:r + 8, 128:], even, axis=1)
                 squeezed[i, pl.ds(r, 8), :] = jnp.where(lane128 < 64, low, high)
             block = squeezed[i, pl.ds(0, cy, stride=2), :] + squeezed[i, pl.ds(1, cy, stride=2), :]
-            group[kind, 1, i, pl.ds(pl.multiple_of(gy * cy, 8), cy), :] = 0.125 * block
+            group[kind, i, pl.ds(pl.multiple_of(all_y + gy * cy, 8), cy), :] = 0.125 * block
 
     coarsen(
         [cond[first + 2 * i, pl.ds(0, ny), :] + cond[first + 2 * i + 1, pl.ds(0, ny), :]
          for i in range(cx)],
         0,
     )
-    load_owners.wait()
-    for c in range(n_gy):
-        holders[1, c] = jnp.full((8, cz), owners_ref[0, c].astype(jnp.float32))
 
     row = lax.broadcasted_iota(jnp.int32, (rows, 1), 0)
     y = gy * ny + jnp.where(row < ny + HALF, row, row - rows)
@@ -248,29 +266,32 @@
     weigh([first - 2, first - 1, first, last - 1, last, last + 1])
     with jax.named_scope("start_coarse_cond"):
         gather_start(0)
-    for dx in (-1, 1):
-        @pl.when(exists(dx, 0))
-        def _():
-            tell(dx).start()
-
     def defect(i, values, flux, keep=rows):
         at = pl.ds(0, keep)
         lhs = cond[i, at] * blend(values[i - 1], values[i], values[i + 1], keep)
         rhs = blend(flux[i - 1], flux[i], flux[i + 1], keep)
         return source[i, at] - diag2[i, at] * values[i][:keep] + lhs + rhs
 
+    values, flux, smooth = {}, {}, {}
+
+    def first_sweep(at):
+        for i in at:
+            values[i] = weight[i] * source[i]
+            flux[i] = cond[i] * values[i]
+
+    def second_sweep(at):
+        for i in at:
+            smooth[i] = values[i] + weight[i] * defect(i, values, flux)
+
     load_source.wait()
     with jax.named_scope("wait_source_rows"):
         receive(SOURCE, True)
+    first_sweep(range(first, last))
+    second_sweep(range(first + 1, last - 1))
     with jax.named_scope("wait_source_planes"):
         receive(SOURCE, False)
-    values, flux = {}, {}
-    for i in range(first - 2, last + 2):
-        values[i] = weight[i] * source[i]
-        flux[i] = cond[i] * values[i]
-    smooth = {}
-    for i in range(first - 1, last + 1):
-        smooth[i] = values[i] + weight[i] * defect(i, values, flux)
+    first_sweep((first - 2, first - 1, last, last + 1))
+    second_sweep((first - 1, first, last - 1, last))
     flux = {i: cond[i] * smooth[i] for i in smooth}
     pairs = []
     for i in range(cx):
@@ -283,7 +304,6 @@
         iterate[i, pl.ds(0, ny), :] = smooth[i][:ny]
     send(ITERATE)
 
-    all_y = n_gy * cy
     crow = lax.broadcasted_iota(jnp.int32, (all_y, cz), 0)
     clane = lax.broadcasted_iota(jnp.int32, (1, cz), 1)
     cz_low = jnp.where(clane == 0, 0.0, 0.5)
@@ -303,15 +323,12 @@
         return jnp.sum(whole, keepdims=True)
 
     with jax.named_scope("wait_holders"):
-        for dx in (-1, 1):
-            @pl.when(exists(-dx, 0))
-            def _():
-                tell(dx).wait_recv()
+        by_neighbours(lambda a, b: wait(holders.at[pl.ds(0, a)], recv_sem.at[8]))
     with jax.named_scope("wait_coarse_cond"):
         gather_wait(0)
     slabs = []
     for g in range(3):
-        held = [holders[g, c, pl.ds(0, 1), :] for c in range(n_gy)]
+        held = [holders[g, pl.ds(c, 1), :] for c in range(n_gy)]
         same = lambda a, b: jnp.where(held[a] == held[b], 1.0, 0.0)
         y_low = jnp.where(crow == 0, 0.0, 0.5)
         y_high = jnp.where(crow == all_y - 1, 0.0, 0.5)
@@ -319,7 +336,7 @@
             tied = 0.5 * same(c - 1, c)
             y_low = jnp.where(crow == c * cy, tied, y_low)
             y_high = jnp.where(crow == c * cy - 1, tied, y_high)
-        k = [group[0, g, i] for i in range(cx)]
+        k = [group[0, i, pl.ds(g * all_y, all_y), :] for i in range(cx)]
         mixed = coarse_blend(k, y_low, y_high)
         diag = [MASS_TERM + 1.5 * a + 0.25 * b for a, b in zip(k, mixed)]
         step = [RELAX_WEIGHT / d for d in diag]
@@ -338,7 +355,7 @@
         gather_wait(1)
     e = []
     for g, s in enumerate(slabs):
-        s["res"] = [group[1, g, i] for i in range(cx)]
+        s["res"] = [group[1, i, pl.ds(g * all_y, all_y), :] for i in range(cx)]
         s["start"] = [a * b for a, b in zip(s["step"], s["res"])]
         e.append(s["start"])
     for _ in range(COARSE_SWEEPS - 1):
@@ -406,17 +423,7 @@
         out_ref[i] = values[first + i][:ny]
 
     with jax.named_scope("wait_sends"):
-        for kind in range(3):
-            finish(kind)
-        for dx in (-1, 1):
-            @pl.when(exists(dx, 0))
-            def _():
-                tell(dx).wait_send()
-        for kind in range(2):
-            for dx, off in near_slabs:
-                @pl.when(exists(dx, 0))
-                def _():
-                    gather(kind, dx, off).wait_send()
+        by_neighbours(finish)
 
 
 def on_device(source, region, permeability, owners, *, n_gx, n_gy):
@@ -433,23 +440,15 @@
             pltpu.SMEM((1, n_gy), jnp.int32),
             pltpu.VMEM((1, permeability.shape[0]), f32),
             pltpu.VMEM((planes, ny + 8, nz), jnp.int32),
-            pltpu.VMEM((planes, ny + 8, nz), f32),
-            pltpu.VMEM((planes, ny + 8, nz), f32),
-            pltpu.VMEM((planes, ny + 8, nz), f32),
-            pltpu.VMEM((planes, ny + 8, nz), f32),
-            pltpu.VMEM((planes, ny + 8, nz), f32),
-            pltpu.VMEM((2, 3, cx, all_y, cz), f32),
-            pltpu.VMEM((3, n_gy, 8, cz), f32),
+            pltpu.VMEM((7 * planes, ny + 8, nz), f32),
+            pltpu.VMEM((2, cx, 3 * all_y, cz), f32),
+            pltpu.VMEM((3, 8, cz), f32),
             pltpu.VMEM((cx, ny, cz), f32),
             pltpu.VMEM((cx + 2, all_y + 16, cz), f32),
             pltpu.VMEM((cx + 2, ny, cz), f32),
             pltpu.VMEM((cx + 2, ny + 8, nz), f32),
-            pltpu.SemaphoreType.DMA((3, 8)),
-            pltpu.SemaphoreType.DMA((3, 8)),
-            pltpu.SemaphoreType.DMA((2, 3, n_gy)),
-            pltpu.SemaphoreType.DMA((2, 3, n_gy)),
-            pltpu.SemaphoreType.DMA((2,)),
-            pltpu.SemaphoreType.DMA((2,)),
+            pltpu.SemaphoreType.DMA((4,)),
+            pltpu.SemaphoreType.DMA((9,)),
             pltpu.SemaphoreType.DMA((4,)),
         ],
         compiler_params=pltpu.CompilerParams(

time: 16.3 us -> 15.6 us (0.957)
  Pallas kernels: 15.5 us -> 14.8 us
    pallas_call x1, Pallas kernels: 15.5 us -> 14.8 us  [on_device(): pl.pallas_call(functools.partial(kernel, n_gx, n_gy), out_shape=jax.Shape...]
where the time goes in v2:
time: 15.6 us; the launch traced here: 15.4 us
  Pallas kernels  14.8 us (95%)
  local copies, waits for them, and re-layouts  0.66 us (4%)
    pallas_call x1, Pallas kernels, on_device(): pl.pallas_call(functools.partial(kernel, n_gx, n_gy), out_shape=jax.Shape...  14.8 us
    unnamed x1, local copies, waits for them, and re-layouts  0.66 us

profile of v2, /device:TPU:1, one launch (start us, length us, event | category | flops | bytes accessed | tf_op | source)
XLA Modules:
  0.0 15.4 jit_solution(5090639119716039047)
XLA Ops:
  0.0 14.8 %shard_map.46 = f32[4,32,256]{2,1,0:T(8,128)S(1)} custom-call(s32[1,2]{1,0:T(1,128)} %owners_in.1, f32[1,64]{1,0:T(1,128)} %bitcast.1, f32[4,32,256]{2,1,0:T(8,128)} %source_ref.1, s32[4,32,256]{2,1,0:T(8,128)} %region_ref.1), custom_call_target="tpu_custom_call" | custom-call | tf_op jit(solution)/shard_map/pallas_call | solution.py:434
  14.8 0.7 %copy.6 = f32[4,32,256]{2,1,0:T(8,128)} copy(f32[4,32,256]{2,1,0:T(8,128)S(1)} %shard_map.46) | data formatting | bytes 262144

commit v3 on v2

--- a/solution.py
+++ b/solution.py
@@ -16,14 +16,17 @@
 WIDE = 3
 HALF = 4
 REGION, SOURCE, ITERATE = 0, 1, 2
-WIDTHS = (3, 2, 2)
+EDGE = 2
+BESIDE = (2, 1, 2)
+CORNER = ((3, HALF), (2, EDGE), (2, HALF))
+STRIP = (3, 2)
 STEPS = ((-1, -1), (1, -1), (-1, 1), (1, 1), (0, -1), (0, 1), (-1, 0), (1, 0))
 
 
 def kernel(
     n_gx, n_gy,
     owners_in, table_in, source_ref, region_ref, out_ref,
-    owners_ref, table_ref, labels, store, group, holders, squeezed, whole_corr, spread, wide,
+    owners_ref, table_ref, labels, store, shipped, group, holders, squeezed, whole_corr, spread, wide,
     send_sem, recv_sem, in_sem,
 ):
     nx, ny, nz = out_ref.shape
@@ -45,6 +48,13 @@
         (dx, off) for dx in (-1, 1, 0) for off in reversed(range(n_gy)) if (dx, off) != (0, 0)
     ]
 
+    nowhere = table_ref.shape[1]
+    for i in range(planes):
+        if i in (0, planes - 1):
+            labels[i] = jnp.full((ny + 8, nz), nowhere, jnp.int32)
+        else:
+            labels[i, pl.ds(ny, 8), :] = jnp.full((8, nz), nowhere, jnp.int32)
+
     barrier = pltpu.get_barrier_semaphore()
     count = jnp.int32(0)
     for dx, off in near_slabs:
@@ -71,33 +81,58 @@
     load_source.start()
     load_owners.start()
 
-    def landing(kind, dx, dy):
-        w = WIDTHS[kind]
-        start, size = {0: (first, nx), -1: (last, w), 1: (first - w, w)}[dx]
-        row, high = {0: (0, ny), -1: (ny, HALF), 1: (ny + HALF, HALF)}[dy]
-        return fields[kind].at[pl.ds(start, size), pl.ds(row, high)]
-
-    def remote(kind, which):
-        dx, dy = STEPS[which]
-        w = WIDTHS[kind]
+    def box(kind, dx, dy):
+        if dx == 0:
+            w, high = nx, HALF
+        elif dy == 0:
+            w, high = BESIDE[kind], ny
+        else:
+            w, high = CORNER[kind]
+        plane = nx - w if dx > 0 else 0
+        land = {0: first, -1: last, 1: first - w}[dx]
+        row = ny - high if dy > 0 else 0
+        to = {0: 0, -1: ny, 1: ny + 8 - high}[dy]
+        return (plane, w, row, high), (land, w, to, high)
+
+    def move(kind, dx, dy, here, there):
+        plane, w, row, high = here
         base = first if kind == ITERATE else 0
-        start, size = {0: (0, nx), -1: (0, w), 1: (nx - w, w)}[dx]
-        row, high = {0: (0, ny), -1: (0, HALF), 1: (ny - HALF, HALF)}[dy]
         origin = (region_ref, source_ref, iterate)[kind]
+        land, _, to, _ = there
         return pltpu.make_async_remote_copy(
-            src_ref=origin.at[pl.ds(base + start, size), pl.ds(row, high)],
-            dst_ref=landing(kind, dx, dy),
+            src_ref=origin.at[pl.ds(base + plane, w), pl.ds(row, high)],
+            dst_ref=fields[kind].at[pl.ds(land, w), pl.ds(to, high)],
             send_sem=send_sem.at[abs(dx)],
             recv_sem=recv_sem.at[2 * kind + abs(dx)],
             device_id=(gx + dx, gy + dy),
             device_id_type=MESH,
         )
 
+    def strips(kind, dx):
+        far = STRIP[kind]
+        plane, land = (nx - far, first - far) if dx > 0 else (far - 1, last + far - 1)
+        for row in (0, ny - EDGE):
+            yield move(kind, dx, 0, (plane, 1, row, EDGE), (land, 1, row, EDGE))
+
+    def ship(dx):
+        side = (1 - dx) // 2
+        return pltpu.make_async_remote_copy(
+            src_ref=shipped.at[2 + side],
+            dst_ref=shipped.at[side],
+            send_sem=send_sem.at[1],
+            recv_sem=recv_sem.at[2 * SOURCE + 1],
+            device_id=(gx + dx, gy),
+            device_id_type=MESH,
+        )
+
     def send(kind):
-        for which, (dx, dy) in enumerate(STEPS):
+        for dx, dy in STEPS:
             @pl.when(exists(dx, dy))
             def _():
-                remote(kind, which).start()
+                move(kind, dx, dy, *box(kind, dx, dy)).start()
+                if dy == 0 and kind != ITERATE:
+                    for strip in strips(kind, dx):
+                        strip.start()
 
     def by_neighbours(act):
         for a in (1, 2):
@@ -116,16 +151,20 @@
         high = next(r for r in (40, 32, 24, 16, 8, HALF) if n % r == 0 and r <= store.shape[1])
         return store.at[pl.ds(0, n // high), pl.ds(0, high)]
 
+    def beside(kind, b):
+        n = BESIDE[kind] * ny + b * CORNER[kind][0] * CORNER[kind][1]
+        return n + {REGION: 2 * EDGE, SOURCE: 2 * EDGE + ny, ITERATE: 0}[kind]
+
     def receive(kind, inner):
         def act(a, b):
-            n = nx * b * HALF if inner else a * WIDTHS[kind] * (ny + b * HALF)
+            n = nx * b * HALF if inner else a * beside(kind, b)
             wait(of_rows(n), recv_sem.at[2 * kind + 1 - inner])
 
         by_neighbours(act)
 
     def finish(a, b):
         wait(of_rows(3 * nx * b * HALF), send_sem.at[0])
-        wait(of_rows(sum(WIDTHS) * a * (ny + b * HALF)), send_sem.at[1])
+        wait(of_rows(a * sum(beside(kind, b) for kind in range(3))), send_sem.at[1])
         wait(group.at[:, :, pl.ds(0, (a * n_gy + n_gy - 1) * cy)], send_sem.at[2])
         wait(holders.at[pl.ds(0, a)], send_sem.at[3])
 
@@ -162,17 +201,20 @@
             group.at[kind, :, pl.ds(0, (a * n_gy + n_gy - 1) * cy)], recv_sem.at[6 + kind]
         ))
 
-    for dx, dy in STEPS:
-        @pl.when(jnp.logical_not(exists(-dx, -dy)))
+    for dy in (-1, 1):
+        @pl.when(jnp.logical_not(exists(0, -dy)))
         def _():
-            ref = landing(REGION, dx, dy)
-            ref[...] = jnp.full(ref.shape, table_ref.shape[1], jnp.int32)
-            for kind in (SOURCE, ITERATE):
-                ref = landing(kind, dx, dy)
-                ref[...] = jnp.zeros(ref.shape, jnp.float32)
+            at = pl.ds(ny if dy < 0 else ny + HALF, HALF)
+            for ref in (source, iterate):
+                ref[:, at, :] = jnp.zeros((planes, HALF, nz), jnp.float32)
     for dx in (-1, 1):
         @pl.when(jnp.logical_not(exists(-dx, 0)))
         def _():
+            at = pl.ds(last if dx < 0 else 0, WIDE)
+            labels[at] = jnp.full((WIDE, ny + 8, nz), nowhere, jnp.int32)
+            for ref in (source, iterate):
+                ref[at] = jnp.zeros((WIDE, ny + 8, nz), jnp.float32)
+            shipped[(1 - dx) // 2] = jnp.zeros((ny, nz), jnp.float32)
             for kind in range(2):
                 ref = group.at[kind, :, pl.ds((1 - dx) * all_y, all_y)]
                 ref[...] = jnp.zeros(ref.shape, jnp.float32)
@@ -236,6 +278,18 @@
             block = squeezed[i, pl.ds(0, cy, stride=2), :] + squeezed[i, pl.ds(1, cy, stride=2), :]
             group[kind, i, pl.ds(pl.multiple_of(all_y + gy * cy, 8), cy), :] = 0.125 * block
 
+    load_source.wait()
+    for dx, i in ((1, last - EDGE), (-1, first + EDGE - 1)):
+        mine = cond[i, pl.ds(0, ny), :]
+        mixed = blend(cond[i - 1], cond[i], cond[i + 1], ny)
+        shipped[2 + (1 - dx) // 2] = (
+            RELAX_WEIGHT * source[i, pl.ds(0, ny), :] / (MASS_TERM + 6.0 * mine + mixed)
+        )
+
+        @pl.when(exists(dx, 0))
+        def _():
+            ship(dx).start()
+
     coarsen(
         [cond[first + 2 * i, pl.ds(0, ny), :] + cond[first + 2 * i + 1, pl.ds(0, ny), :]
          for i in range(cx)],
@@ -246,8 +300,8 @@
     y = gy * ny + jnp.where(row < ny + HALF, row, row - rows)
     in_y = jnp.where((y >= 0) & (y < n_gy * ny), RELAX_WEIGHT, 0.0)
 
-    def weigh(planes):
-        for i in planes:
+    def weigh(at):
+        for i in at:
             mine = cond[i]
             mixed = blend(cond[i - 1], mine, cond[i + 1])
             x = gx * nx + (i - first)
@@ -277,13 +331,16 @@
     def first_sweep(at):
         for i in at:
             values[i] = weight[i] * source[i]
+            if i in (first - EDGE, last + EDGE - 1):
+                side = int(i > first)
+                far = jnp.concatenate([shipped[side], jnp.zeros((8, nz), jnp.float32)])
+                values[i] = jnp.where((row > 0) & (row < ny - 1), far, values[i])
             flux[i] = cond[i] * values[i]
 
     def second_sweep(at):
         for i in at:
             smooth[i] = values[i] + weight[i] * defect(i, values, flux)
 
-    load_source.wait()
     with jax.named_scope("wait_source_rows"):
         receive(SOURCE, True)
     first_sweep(range(first, last))
@@ -441,6 +498,7 @@
             pltpu.VMEM((1, permeability.shape[0]), f32),
             pltpu.VMEM((planes, ny + 8, nz), jnp.int32),
             pltpu.VMEM((7 * planes, ny + 8, nz), f32),
+            pltpu.VMEM((4, ny, nz), f32),
             pltpu.VMEM((2, cx, 3 * all_y, cz), f32),
             pltpu.VMEM((3, 8, cz), f32),
             pltpu.VMEM((cx, ny, cz), f32),

time: 15.6 us -> 15 us (0.962)
  Pallas kernels: 14.8 us -> 14.2 us
    pallas_call x1, Pallas kernels: 14.8 us -> 14.2 us  [on_device(): pl.pallas_call(functools.partial(kernel, n_gx, n_gy), out_shape=jax.Shape...]
where the time goes in v3:
time: 15 us; the launch traced here: 14.9 us
  Pallas kernels  14.2 us (95%)
  local copies, waits for them, and re-layouts  0.66 us (4%)
    pallas_call x1, Pallas kernels, on_device(): pl.pallas_call(functools.partial(kernel, n_gx, n_gy), out_shape=jax.Shape...  14.2 us
    unnamed x1, local copies, waits for them, and re-layouts  0.66 us

profile of v3, /device:TPU:1, one launch (start us, length us, event | category | flops | bytes accessed | tf_op | source)
XLA Modules:
  0.0 14.9 jit_solution(4989481540320776911)
XLA Ops:
  0.0 14.2 %shard_map.46 = f32[4,32,256]{2,1,0:T(8,128)S(1)} custom-call(s32[1,2]{1,0:T(1,128)} %owners_in.1, f32[1,64]{1,0:T(1,128)} %bitcast.1, f32[4,32,256]{2,1,0:T(8,128)} %source_ref.1, s32[4,32,256]{2,1,0:T(8,128)} %region_ref.1), custom_call_target="tpu_custom_call" | custom-call | tf_op jit(solution)/shard_map/pallas_call | solution.py:491
  14.2 0.7 %copy.6 = f32[4,32,256]{2,1,0:T(8,128)} copy(f32[4,32,256]{2,1,0:T(8,128)S(1)} %shard_map.46) | data formatting | bytes 262144

commit v4 on v3

--- a/solution.py
+++ b/solution.py
@@ -27,7 +27,7 @@
     n_gx, n_gy,
     owners_in, table_in, source_ref, region_ref, out_ref,
     owners_ref, table_ref, labels, store, shipped, group, holders, squeezed, whole_corr, spread, wide,
-    send_sem, recv_sem, in_sem,
+    send_sem, recv_sem, in_sem, ready_sem,
 ):
     nx, ny, nz = out_ref.shape
     cx, cy, cz = nx // 2, ny // 2, nz // 2
@@ -58,6 +58,8 @@
     barrier = pltpu.get_barrier_semaphore()
     count = jnp.int32(0)
     for dx, off in near_slabs:
+        if dx != 0 and off != 0:
+            continue
         near = exists(dx, 0)
 
         @pl.when(near)
@@ -125,9 +127,20 @@
             device_id_type=MESH,
         )
 
-    def send(kind):
+    def far(dx):
+        return lax.rem(gx + (dx + 1) // 2, 4) == 0
+
+    def send(kind, corners=(False, True), late=None):
         for dx, dy in STEPS:
-            @pl.when(exists(dx, dy))
+            if (dx * dy != 0) not in corners:
+                continue
+            now = exists(dx, dy)
+            if late is not None and dx != 0:
+                now = now & (far(dx) == late)
+            elif late:
+                continue
+
+            @pl.when(now)
             def _():
                 move(kind, dx, dy, *box(kind, dx, dy)).start()
                 if dy == 0 and kind != ITERATE:
@@ -223,8 +236,12 @@
 
     with jax.named_scope("wait_neighbours"):
         pl.semaphore_wait(barrier, count)
-    send(REGION)
-    send(SOURCE)
+    send(REGION, (False,))
+    for off in range(1, n_gy):
+        pl.semaphore_signal(
+            ready_sem, inc=1, device_id=(gx, lax.rem(gy + off, n_gy)), device_id_type=MESH
+        )
+    send(SOURCE, (False,), False)
 
     load_owners.wait()
     eight = lax.broadcasted_iota(jnp.int32, (8, cz), 0)
@@ -253,16 +270,21 @@
 
     look_up(range(first, last), range(0, ny, 8))
 
-    lane = lax.broadcasted_iota(jnp.int32, (1, nz), 1)
-    z_low = jnp.where(lane == 0, 0.0, 0.5)
-    z_high = jnp.where(lane == nz - 1, 0.0, 0.5)
     rows = ny + 8
 
     def blend(a, b, c, keep=rows):
         u = b + 0.5 * (a + c)
         u = u + 0.5 * (pltpu.roll(u, 1, 0) + pltpu.roll(u, rows - 1, 0))
         u = u[:keep]
-        return u + z_low * pltpu.roll(u, 1, 1) + z_high * pltpu.roll(u, nz - 1, 1)
+        parts = [u[:, c:c + 128] for c in range(0, nz, 128)]
+        up = [pltpu.roll(p, 1, 1) for p in parts]
+        down = [pltpu.roll(p, 127, 1) for p in parts]
+        mixed = []
+        for j, p in enumerate(parts):
+            low = jnp.where(lane128[:1] == 0, up[j - 1] if j else 0.0, up[j])
+            high = jnp.where(lane128[:1] == 127, down[j + 1] if j + 1 < len(parts) else 0.0, down[j])
+            mixed.append(p + 0.5 * (low + high))
+        return jnp.concatenate(mixed, axis=1)
 
     lane128 = lax.broadcasted_iota(jnp.int32, (8, 128), 1)
     even = lax.rem(2 * lane128, jnp.int32(128))
@@ -289,6 +311,12 @@
         @pl.when(exists(dx, 0))
         def _():
             ship(dx).start()
+
+    with jax.named_scope("wait_corners"):
+        pl.semaphore_wait(ready_sem, n_gy - 1)
+    send(REGION, (True,))
+    send(SOURCE, (True,))
+    send(SOURCE, (False,), True)
 
     coarsen(
         [cond[first + 2 * i, pl.ds(0, ny), :] + cond[first + 2 * i + 1, pl.ds(0, ny), :]
@@ -437,12 +465,22 @@
         ratios.append(shares)
     for slot, (g, i) in enumerate(keep_planes):
         whole_corr[slot, pl.ds(0, 8), :] = jnp.zeros((8, cz), jnp.float32)
+        whole_corr[slot, pl.ds(8, all_y), :] = e[g][i]
         whole_corr[slot, pl.ds(8 + all_y, 8), :] = jnp.zeros((8, cz), jnp.float32)
+
+    sub = lax.broadcasted_iota(jnp.int32, (8, nz), 0)
+
+    def of_column(g, column):
+        found = jnp.zeros((1, 1), jnp.float32)
         for c in range(n_gy):
-            whole_corr[slot, pl.ds(8 + c * cy, cy), :] = e[g][i][c * cy:(c + 1) * cy] + ratios[g][c]
-
-    sub = lax.broadcasted_iota(jnp.int32, (8, cz), 0)
-    for i in range(cx + 2):
+            found = jnp.where(column == c, ratios[g][c], found)
+        return jnp.broadcast_to(found, (8, nz))
+
+    shifts = [
+        (of_column(g, gy), jnp.where(sub < HALF, of_column(g, gy + 1), of_column(g, gy - 1)))
+        for g in range(3)
+    ]
+    for i, (g, _) in enumerate(keep_planes):
         mine = whole_corr[i, pl.ds(pl.multiple_of(8 + gy * cy, 8), cy), :]
         below = whole_corr[i, pl.ds(pl.multiple_of(gy * cy, 8), 8), :]
         above = whole_corr[i, pl.ds(pl.multiple_of(8 + gy * cy + cy, 8), 8), :]
@@ -453,14 +491,14 @@
                 tile = spread[i, pl.ds(r, 8), :]
             else:
                 tile = jnp.where(
-                    sub < HALF,
+                    sub[:, :cz] < HALF,
                     jnp.broadcast_to(above[:1], (8, cz)),
                     jnp.broadcast_to(below[7:], (8, cz)),
                 )
-            for part in range(2):
-                wide[i, pl.ds(r, 8), pl.ds(128 * part, 128)] = jnp.take_along_axis(
-                    tile, half_of + 64 * part, axis=1
-                )
+            halves = [
+                jnp.take_along_axis(tile, half_of + 64 * part, axis=1) for part in range(2)
+            ]
+            wide[i, pl.ds(r, 8), :] = jnp.concatenate(halves, axis=1) + shifts[g][int(r >= ny)]
     with jax.named_scope("wait_iterate_rows"):
         receive(ITERATE, True)
     with jax.named_scope("wait_iterate_planes"):
@@ -508,6 +546,7 @@
             pltpu.SemaphoreType.DMA((4,)),
             pltpu.SemaphoreType.DMA((9,)),
             pltpu.SemaphoreType.DMA((4,)),
+            pltpu.SemaphoreType.REGULAR,
         ],
         compiler_params=pltpu.CompilerParams(
             collective_id=0, has_side_effects=True, vmem_limit_bytes=56328192

time: 15 us -> 14.6 us (0.973)
  Pallas kernels: 14.2 us -> 13.8 us
    pallas_call x1, Pallas kernels: 14.2 us -> 13.8 us  [on_device(): pl.pallas_call(functools.partial(kernel, n_gx, n_gy), out_shape=jax.Shape...]
where the time goes in v4:
time: 14.6 us; the launch traced here: 14.5 us
  Pallas kernels  13.8 us (95%)
  local copies, waits for them, and re-layouts  0.66 us (5%)
    pallas_call x1, Pallas kernels, on_device(): pl.pallas_call(functools.partial(kernel, n_gx, n_gy), out_shape=jax.Shape...  13.8 us
    unnamed x1, local copies, waits for them, and re-layouts  0.66 us

profile of v4, /device:TPU:1, one launch (start us, length us, event | category | flops | bytes accessed | tf_op | source)
XLA Modules:
  0.0 14.5 jit_solution(3842403193843557857)
XLA Ops:
  0.0 13.8 %shard_map.46 = f32[4,32,256]{2,1,0:T(8,128)S(1)} custom-call(s32[1,2]{1,0:T(1,128)} %owners_in.1, f32[1,64]{1,0:T(1,128)} %bitcast.1, f32[4,32,256]{2,1,0:T(8,128)} %source_ref.1, s32[4,32,256]{2,1,0:T(8,128)} %region_ref.1), custom_call_target="tpu_custom_call" | custom-call | tf_op jit(solution)/shard_map/pallas_call | solution.py:529
  13.8 0.7 %copy.6 = f32[4,32,256]{2,1,0:T(8,128)} copy(f32[4,32,256]{2,1,0:T(8,128)S(1)} %shard_map.46) | data formatting | bytes 262144

commit v5 on v4

--- a/solution.py
+++ b/solution.py
@@ -27,7 +27,7 @@
     n_gx, n_gy,
     owners_in, table_in, source_ref, region_ref, out_ref,
     owners_ref, table_ref, labels, store, shipped, group, holders, squeezed, whole_corr, spread, wide,
-    send_sem, recv_sem, in_sem, ready_sem,
+    send_sem, recv_sem, in_sem, ready_sem, pace_sem,
 ):
     nx, ny, nz = out_ref.shape
     cx, cy, cz = nx // 2, ny // 2, nz // 2
@@ -129,6 +129,12 @@
 
     def far(dx):
         return lax.rem(gx + (dx + 1) // 2, 4) == 0
+
+    def to_group(sem):
+        for off in range(1, n_gy):
+            pl.semaphore_signal(
+                sem, inc=1, device_id=(gx, lax.rem(gy + off, n_gy)), device_id_type=MESH
+            )
 
     def send(kind, corners=(False, True), late=None):
         for dx, dy in STEPS:
@@ -237,10 +243,7 @@
     with jax.named_scope("wait_neighbours"):
         pl.semaphore_wait(barrier, count)
     send(REGION, (False,))
-    for off in range(1, n_gy):
-        pl.semaphore_signal(
-            ready_sem, inc=1, device_id=(gx, lax.rem(gy + off, n_gy)), device_id_type=MESH
-        )
+    to_group(ready_sem)
     send(SOURCE, (False,), False)
 
     load_owners.wait()
@@ -308,7 +311,7 @@
             RELAX_WEIGHT * source[i, pl.ds(0, ny), :] / (MASS_TERM + 6.0 * mine + mixed)
         )
 
-        @pl.when(exists(dx, 0))
+        @pl.when(exists(dx, 0) & jnp.logical_not(far(dx)))
         def _():
             ship(dx).start()
 
@@ -316,8 +319,6 @@
         pl.semaphore_wait(ready_sem, n_gy - 1)
     send(REGION, (True,))
     send(SOURCE, (True,))
-    send(SOURCE, (False,), True)
-
     coarsen(
         [cond[first + 2 * i, pl.ds(0, ny), :] + cond[first + 2 * i + 1, pl.ds(0, ny), :]
          for i in range(cx)],
@@ -336,6 +337,15 @@
             in_x = jnp.where((x >= 0) & (x < n_gx * nx), 1.0, 0.0)
             weight[i] = (in_y * in_x) / (MASS_TERM + 6.0 * mine + mixed)
             diag2[i] = MASS_TERM + 8.0 * mine + mixed
+
+    with jax.named_scope("pace"):
+        to_group(pace_sem)
+        pl.semaphore_wait(pace_sem, n_gy - 1)
+    send(SOURCE, (False,), True)
+    for dx in (-1, 1):
+        @pl.when(exists(dx, 0) & far(dx))
+        def _():
+            ship(dx).start()
 
     with jax.named_scope("wait_region_rows"):
         receive(REGION, True)
@@ -547,6 +557,7 @@
             pltpu.SemaphoreType.DMA((9,)),
             pltpu.SemaphoreType.DMA((4,)),
             pltpu.SemaphoreType.REGULAR,
+            pltpu.SemaphoreType.REGULAR,
         ],
         compiler_params=pltpu.CompilerParams(
             collective_id=0, has_side_effects=True, vmem_limit_bytes=56328192

time: 14.6 us -> 13.9 us (0.952)
  Pallas kernels: 13.8 us -> 13.1 us
    pallas_call x1, Pallas kernels: 13.8 us -> 13.1 us  [on_device(): pl.pallas_call(functools.partial(kernel, n_gx, n_gy), out_shape=jax.Shape...]
where the time goes in v5:
time: 13.9 us; the launch traced here: 13.7 us
  Pallas kernels  13.1 us (94%)
  local copies, waits for them, and re-layouts  0.66 us (5%)
    pallas_call x1, Pallas kernels, on_device(): pl.pallas_call(functools.partial(kernel, n_gx, n_gy), out_shape=jax.Shape...  13.1 us
    unnamed x1, local copies, waits for them, and re-layouts  0.66 us

profile of v5, /device:TPU:1, one launch (start us, length us, event | category | flops | bytes accessed | tf_op | source)
XLA Modules:
  0.0 13.7 jit_solution(10536352947512699774)
XLA Ops:
  0.0 13.1 %shard_map.46 = f32[4,32,256]{2,1,0:T(8,128)S(1)} custom-call(s32[1,2]{1,0:T(1,128)} %owners_in.1, f32[1,64]{1,0:T(1,128)} %bitcast.1, f32[4,32,256]{2,1,0:T(8,128)} %source_ref.1, s32[4,32,256]{2,1,0:T(8,128)} %region_ref.1), custom_call_target="tpu_custom_call" | custom-call | tf_op jit(solution)/shard_map/pallas_call | solution.py:539
  13.1 0.7 %copy.6 = f32[4,32,256]{2,1,0:T(8,128)} copy(f32[4,32,256]{2,1,0:T(8,128)S(1)} %shard_map.46) | data formatting | bytes 262144

commit v6 on v5

--- a/solution.py
+++ b/solution.py
@@ -98,14 +98,12 @@
 
     def move(kind, dx, dy, here, there):
         plane, w, row, high = here
-        base = first if kind == ITERATE else 0
-        origin = (region_ref, source_ref, iterate)[kind]
         land, _, to, _ = there
         return pltpu.make_async_remote_copy(
-            src_ref=origin.at[pl.ds(base + plane, w), pl.ds(row, high)],
+            src_ref=fields[kind].at[pl.ds(first + plane, w), pl.ds(row, high)],
             dst_ref=fields[kind].at[pl.ds(land, w), pl.ds(to, high)],
             send_sem=send_sem.at[abs(dx)],
-            recv_sem=recv_sem.at[2 * kind + abs(dx)],
+            recv_sem=recv_sem.at[9 if kind == REGION and dx * dy else 2 * kind + abs(dx)],
             device_id=(gx + dx, gy + dy),
             device_id_type=MESH,
         )
@@ -176,7 +174,7 @@
 
     def receive(kind, inner):
         def act(a, b):
-            n = nx * b * HALF if inner else a * beside(kind, b)
+            n = nx * b * HALF if inner else a * beside(kind, 0 if kind == REGION else b)
             wait(of_rows(n), recv_sem.at[2 * kind + 1 - inner])
 
         by_neighbours(act)
@@ -242,8 +240,11 @@
 
     with jax.named_scope("wait_neighbours"):
         pl.semaphore_wait(barrier, count)
+    with jax.named_scope("wait_own_region"):
+        load_region.wait()
     send(REGION, (False,))
     to_group(ready_sem)
+    load_source.wait()
     send(SOURCE, (False,), False)
 
     load_owners.wait()
@@ -258,8 +259,6 @@
             tell(dx).start()
 
     load_table.wait()
-    with jax.named_scope("wait_own_region"):
-        load_region.wait()
     regions = table_ref.shape[1]
     pair = jnp.concatenate([table_ref[...], jnp.zeros((1, 128 - regions), jnp.float32)], axis=1)
     table = jnp.broadcast_to(pair, (8, 128))
@@ -303,7 +302,6 @@
             block = squeezed[i, pl.ds(0, cy, stride=2), :] + squeezed[i, pl.ds(1, cy, stride=2), :]
             group[kind, i, pl.ds(pl.multiple_of(all_y + gy * cy, 8), cy), :] = 0.125 * block
 
-    load_source.wait()
     for dx, i in ((1, last - EDGE), (-1, first + EDGE - 1)):
         mine = cond[i, pl.ds(0, ny), :]
         mixed = blend(cond[i - 1], cond[i], cond[i + 1], ny)
@@ -354,7 +352,12 @@
     with jax.named_scope("wait_region_planes"):
         receive(REGION, False)
     edges = [*range(first - WIDE, first), *range(last, last + WIDE)]
-    look_up(edges, range(0, rows, 8))
+    look_up(edges, range(0, ny, 8))
+    with jax.named_scope("wait_region_corners"):
+        by_neighbours(lambda a, b: wait(
+            of_rows(a * b * CORNER[REGION][0] * CORNER[REGION][1]), recv_sem.at[9]
+        ))
+    look_up(edges, (ny,))
     weigh([first - 2, first - 1, first, last - 1, last, last + 1])
     with jax.named_scope("start_coarse_cond"):
         gather_start(0)
@@ -554,7 +557,7 @@
             pltpu.VMEM((cx + 2, ny, cz), f32),
             pltpu.VMEM((cx + 2, ny + 8, nz), f32),
             pltpu.SemaphoreType.DMA((4,)),
-            pltpu.SemaphoreType.DMA((9,)),
+            pltpu.SemaphoreType.DMA((10,)),
             pltpu.SemaphoreType.DMA((4,)),
             pltpu.SemaphoreType.REGULAR,
             pltpu.SemaphoreType.REGULAR,

time: 13.9 us -> 13.8 us (level)
  the two profiles are of different devices: /device:TPU:1 before, /device:TPU:9 now
where the time goes in v6:
time: 13.8 us; the launch traced here: 13.7 us
  Pallas kernels  13 us (94%)
  local copies, waits for them, and re-layouts  0.66 us (5%)
    pallas_call x1, Pallas kernels, on_device(): pl.pallas_call(functools.partial(kernel, n_gx, n_gy), out_shape=jax.Shape...  13 us
    unnamed x1, local copies, waits for them, and re-layouts  0.66 us

profile of v6, /device:TPU:9, one launch (start us, length us, event | category | flops | bytes accessed | tf_op | source)
XLA Modules:
  0.0 13.7 jit_solution(1719637657667041430)
XLA Ops:
  0.0 13.0 %shard_map.46 = f32[4,32,256]{2,1,0:T(8,128)S(1)} custom-call(s32[1,2]{1,0:T(1,128)} %owners_in.1, f32[1,64]{1,0:T(1,128)} %bitcast.1, f32[4,32,256]{2,1,0:T(8,128)} %source_ref.1, s32[4,32,256]{2,1,0:T(8,128)} %region_ref.1), custom_call_target="tpu_custom_call" | custom-call | tf_op jit(solution)/shard_map/pallas_call | solution.py:542
  13.0 0.7 %copy.6 = f32[4,32,256]{2,1,0:T(8,128)} copy(f32[4,32,256]{2,1,0:T(8,128)S(1)} %shard_map.46) | data formatting | bytes 262144

commit v7 on v6

--- a/solution.py
+++ b/solution.py
@@ -26,7 +26,7 @@
 def kernel(
     n_gx, n_gy,
     owners_in, table_in, source_ref, region_ref, out_ref,
-    owners_ref, table_ref, labels, store, shipped, group, holders, squeezed, whole_corr, spread, wide,
+    owners_ref, table_ref, labels, store, shipped, group, holders, squeezed, whole_corr, wide,
     send_sem, recv_sem, in_sem, ready_sem, pace_sem,
 ):
     nx, ny, nz = out_ref.shape
@@ -102,8 +102,10 @@
         return pltpu.make_async_remote_copy(
             src_ref=fields[kind].at[pl.ds(first + plane, w), pl.ds(row, high)],
             dst_ref=fields[kind].at[pl.ds(land, w), pl.ds(to, high)],
-            send_sem=send_sem.at[abs(dx)],
-            recv_sem=recv_sem.at[9 if kind == REGION and dx * dy else 2 * kind + abs(dx)],
+            send_sem=send_sem.at[0],
+            recv_sem=recv_sem.at[
+                5 if kind == REGION and dx * dy else 2 * kind + abs(dx) * (kind != ITERATE)
+            ],
             device_id=(gx + dx, gy + dy),
             device_id_type=MESH,
         )
@@ -119,7 +121,7 @@
         return pltpu.make_async_remote_copy(
             src_ref=shipped.at[2 + side],
             dst_ref=shipped.at[side],
-            send_sem=send_sem.at[1],
+            send_sem=send_sem.at[0],
             recv_sem=recv_sem.at[2 * SOURCE + 1],
             device_id=(gx + dx, gy),
             device_id_type=MESH,
@@ -175,15 +177,19 @@
     def receive(kind, inner):
         def act(a, b):
             n = nx * b * HALF if inner else a * beside(kind, 0 if kind == REGION else b)
-            wait(of_rows(n), recv_sem.at[2 * kind + 1 - inner])
+            if kind == ITERATE:
+                n += nx * b * HALF
+            wait(of_rows(n), recv_sem.at[2 * kind + (not inner and kind != ITERATE)])
 
         by_neighbours(act)
 
+    def group_rows(a):
+        return (a * n_gy + n_gy - 1) * cx * cy * cz // nz
+
     def finish(a, b):
-        wait(of_rows(3 * nx * b * HALF), send_sem.at[0])
-        wait(of_rows(a * sum(beside(kind, b) for kind in range(3))), send_sem.at[1])
-        wait(group.at[:, :, pl.ds(0, (a * n_gy + n_gy - 1) * cy)], send_sem.at[2])
-        wait(holders.at[pl.ds(0, a)], send_sem.at[3])
+        beside_x = a * sum(beside(kind, b) for kind in range(3))
+        wait(of_rows(3 * nx * b * HALF + beside_x), send_sem.at[0])
+        wait(of_rows(2 * group_rows(a) + 8 * a * cz // nz), send_sem.at[1])
 
     def gather(kind, dx, off):
         at = pl.ds(pl.multiple_of(all_y + gy * cy, 8), cy)
@@ -191,7 +197,7 @@
         return pltpu.make_async_remote_copy(
             src_ref=group.at[kind, :, at],
             dst_ref=group.at[kind, :, to],
-            send_sem=send_sem.at[2],
+            send_sem=send_sem.at[1],
             recv_sem=recv_sem.at[6 + kind],
             device_id=(gx + dx, lax.rem(gy + off, n_gy)),
             device_id_type=MESH,
@@ -201,8 +207,8 @@
         return pltpu.make_async_remote_copy(
             src_ref=holders.at[1],
             dst_ref=holders.at[1 - dx],
-            send_sem=send_sem.at[3],
-            recv_sem=recv_sem.at[8],
+            send_sem=send_sem.at[1],
+            recv_sem=recv_sem.at[6],
             device_id=(gx + dx, gy),
             device_id_type=MESH,
         )
@@ -214,8 +220,9 @@
                 gather(kind, dx, off).start()
 
     def gather_wait(kind):
+        told = 0 if kind else 8 * cz // nz
         by_neighbours(lambda a, b: wait(
-            group.at[kind, :, pl.ds(0, (a * n_gy + n_gy - 1) * cy)], recv_sem.at[6 + kind]
+            of_rows(group_rows(a) + a * told), recv_sem.at[6 + kind]
         ))
 
     for dy in (-1, 1):
@@ -294,11 +301,13 @@
 
     def coarsen(pairs, kind):
         for i, pair_sum in enumerate(pairs):
-            total = pair_sum + pltpu.roll(pair_sum, nz - 1, 1)
             for r in range(0, ny, 8):
-                low = jnp.take_along_axis(total[r:r + 8, :128], even, axis=1)
-                high = jnp.take_along_axis(total[r:r + 8, 128:], even, axis=1)
-                squeezed[i, pl.ds(r, 8), :] = jnp.where(lane128 < 64, low, high)
+                halves = (pair_sum[r:r + 8, :128], pair_sum[r:r + 8, 128:])
+                evens = [jnp.take_along_axis(h, even, axis=1) for h in halves]
+                odds = [jnp.take_along_axis(h, even + 1, axis=1) for h in halves]
+                squeezed[i, pl.ds(r, 8), :] = (
+                    jnp.where(lane128 < 64, *evens) + jnp.where(lane128 < 64, *odds)
+                )
             block = squeezed[i, pl.ds(0, cy, stride=2), :] + squeezed[i, pl.ds(1, cy, stride=2), :]
             group[kind, i, pl.ds(pl.multiple_of(all_y + gy * cy, 8), cy), :] = 0.125 * block
 
@@ -355,7 +364,7 @@
     look_up(edges, range(0, ny, 8))
     with jax.named_scope("wait_region_corners"):
         by_neighbours(lambda a, b: wait(
-            of_rows(a * b * CORNER[REGION][0] * CORNER[REGION][1]), recv_sem.at[9]
+            of_rows(a * b * CORNER[REGION][0] * CORNER[REGION][1]), recv_sem.at[5]
         ))
     look_up(edges, (ny,))
     weigh([first - 2, first - 1, first, last - 1, last, last + 1])
@@ -420,8 +429,6 @@
         whole = functools.reduce(jnp.add, [v[c * cy:(c + 1) * cy] for v in planes])
         return jnp.sum(whole, keepdims=True)
 
-    with jax.named_scope("wait_holders"):
-        by_neighbours(lambda a, b: wait(holders.at[pl.ds(0, a)], recv_sem.at[8]))
     with jax.named_scope("wait_coarse_cond"):
         gather_wait(0)
     slabs = []
@@ -446,8 +453,12 @@
             theirs=[0.25 * s for s in step],
             drain=[MASS_TERM + 0.25 * a * (8.0 - b) for a, b in zip(k, ones)],
             same=[[same(a, b)[:, :1] for b in range(n_gy)] for a in range(n_gy)],
-            diag_sum=[total(diag, c) for c in range(n_gy)],
         ))
+        s = slabs[-1]
+        diag_sum = [total(diag, c) for c in range(n_gy)]
+        for line in s["same"]:
+            den = functools.reduce(jnp.add, [a * d for a, d in zip(line, diag_sum)])
+            line[:] = [a / jnp.maximum(den, 1.0) for a in line]
 
     with jax.named_scope("wait_coarse_res"):
         gather_wait(1)
@@ -473,8 +484,7 @@
         shares = []
         for c in range(n_gy):
             num = functools.reduce(jnp.add, [s["same"][c][b] * left[b] for b in range(n_gy)])
-            den = functools.reduce(jnp.add, [s["same"][c][b] * s["diag_sum"][b] for b in range(n_gy)])
-            shares.append(num / jnp.maximum(den, 1.0))
+            shares.append(num)
         ratios.append(shares)
     for slot, (g, i) in enumerate(keep_planes):
         whole_corr[slot, pl.ds(0, 8), :] = jnp.zeros((8, cz), jnp.float32)
@@ -497,27 +507,25 @@
         mine = whole_corr[i, pl.ds(pl.multiple_of(8 + gy * cy, 8), cy), :]
         below = whole_corr[i, pl.ds(pl.multiple_of(gy * cy, 8), 8), :]
         above = whole_corr[i, pl.ds(pl.multiple_of(8 + gy * cy + cy, 8), 8), :]
-        spread[i, pl.ds(0, cy, stride=2), :] = mine
-        spread[i, pl.ds(1, cy, stride=2), :] = mine
-        for r in range(0, rows, 8):
-            if r < ny:
-                tile = spread[i, pl.ds(r, 8), :]
-            else:
-                tile = jnp.where(
-                    sub[:, :cz] < HALF,
-                    jnp.broadcast_to(above[:1], (8, cz)),
-                    jnp.broadcast_to(below[7:], (8, cz)),
-                )
-            halves = [
-                jnp.take_along_axis(tile, half_of + 64 * part, axis=1) for part in range(2)
-            ]
-            wide[i, pl.ds(r, 8), :] = jnp.concatenate(halves, axis=1) + shifts[g][int(r >= ny)]
-    with jax.named_scope("wait_iterate_rows"):
-        receive(ITERATE, True)
+        outer = jnp.where(
+            sub[:, :cz] < HALF,
+            jnp.broadcast_to(above[:1], (8, cz)),
+            jnp.broadcast_to(below[7:], (8, cz)),
+        )
+        for part in range(2):
+            at = half_of + 64 * part
+            for r in range(0, cy, 8):
+                tile = jnp.take_along_axis(mine[r:r + 8], at, axis=1) + shifts[g][0][:, :128]
+                wide[i, part, pl.ds(2 * r, 8, stride=2), :] = tile
+                wide[i, part, pl.ds(2 * r + 1, 8, stride=2), :] = tile
+            wide[i, part, pl.ds(ny, 8), :] = (
+                jnp.take_along_axis(outer, at, axis=1) + shifts[g][1][:, :128]
+            )
     with jax.named_scope("wait_iterate_planes"):
         receive(ITERATE, False)
     values = {
-        i: iterate[i] + wide[(i - first + 2) // 2] for i in range(first - 2, last + 2)
+        i: iterate[i] + jnp.concatenate([wide[(i - first + 2) // 2, part] for part in range(2)], axis=1)
+        for i in range(first - 2, last + 2)
     }
     for sweep in range(POST_SWEEPS):
         reach = POST_SWEEPS - 1 - sweep
@@ -548,16 +556,15 @@
             pltpu.SMEM((1, n_gy), jnp.int32),
             pltpu.VMEM((1, permeability.shape[0]), f32),
             pltpu.VMEM((planes, ny + 8, nz), jnp.int32),
-            pltpu.VMEM((7 * planes, ny + 8, nz), f32),
+            pltpu.VMEM((8 * planes, ny + 8, nz), f32),
             pltpu.VMEM((4, ny, nz), f32),
             pltpu.VMEM((2, cx, 3 * all_y, cz), f32),
             pltpu.VMEM((3, 8, cz), f32),
             pltpu.VMEM((cx, ny, cz), f32),
             pltpu.VMEM((cx + 2, all_y + 16, cz), f32),
-            pltpu.VMEM((cx + 2, ny, cz), f32),
-            pltpu.VMEM((cx + 2, ny + 8, nz), f32),
-            pltpu.SemaphoreType.DMA((4,)),
-            pltpu.SemaphoreType.DMA((10,)),
+            pltpu.VMEM((cx + 2, 2, ny + 8, cz), f32),
+            pltpu.SemaphoreType.DMA((2,)),
+            pltpu.SemaphoreType.DMA((8,)),
             pltpu.SemaphoreType.DMA((4,)),
             pltpu.SemaphoreType.REGULAR,
             pltpu.SemaphoreType.REGULAR,

time: 13.8 us -> 13.7 us (level)
  no operation moved by 1% of the time
where the time goes in v7:
time: 13.7 us; the launch traced here: 13.6 us
  Pallas kernels  12.9 us (94%)
  local copies, waits for them, and re-layouts  0.66 us (5%)
    pallas_call x1, Pallas kernels, on_device(): pl.pallas_call(functools.partial(kernel, n_gx, n_gy), out_shape=jax.Shape...  12.9 us
    unnamed x1, local copies, waits for them, and re-layouts  0.66 us

profile of v7, /device:TPU:9, one launch (start us, length us, event | category | flops | bytes accessed | tf_op | source)
XLA Modules:
  0.0 13.6 jit_solution(2619624933232782335)
XLA Ops:
  0.0 12.9 %shard_map.46 = f32[4,32,256]{2,1,0:T(8,128)S(1)} custom-call(s32[1,2]{1,0:T(1,128)} %owners_in.1, f32[1,64]{1,0:T(1,128)} %bitcast.1, f32[4,32,256]{2,1,0:T(8,128)} %source_ref.1, s32[4,32,256]{2,1,0:T(8,128)} %region_ref.1), custom_call_target="tpu_custom_call" | custom-call | tf_op jit(solution)/shard_map/pallas_call | solution.py:550
  12.9 0.7 %copy.6 = f32[4,32,256]{2,1,0:T(8,128)} copy(f32[4,32,256]{2,1,0:T(8,128)S(1)} %shard_map.46) | data formatting | bytes 262144

commit v8 on v7

--- a/solution.py
+++ b/solution.py
@@ -45,7 +45,7 @@
         return (x >= 0) & (x < n_gx) & (y >= 0) & (y < n_gy)
 
     near_slabs = [
-        (dx, off) for dx in (-1, 1, 0) for off in reversed(range(n_gy)) if (dx, off) != (0, 0)
+        (dx, off) for off in reversed(range(n_gy)) for dx in (-1, 1, 0) if (dx, off) != (0, 0)
     ]
 
     nowhere = table_ref.shape[1]
@@ -215,9 +215,18 @@
 
     def gather_start(kind):
         for dx, off in near_slabs:
-            @pl.when(exists(dx, 0))
-            def _():
+            if not dx:
                 gather(kind, dx, off).start()
+        for dx, off in near_slabs:
+            if dx:
+                @pl.when(exists(dx, 0) & far(dx))
+                def _():
+                    gather(kind, dx, off).start()
+        for dx, off in near_slabs:
+            if dx:
+                @pl.when(exists(dx, 0) & jnp.logical_not(far(dx)))
+                def _():
+                    gather(kind, dx, off).start()
 
     def gather_wait(kind):
         told = 0 if kind else 8 * cz // nz

time: 13.7 us -> 13.7 us (level)
  the two profiles are of different devices: /device:TPU:9 before, /device:TPU:1 now
where the time goes in v8:
time: 13.7 us; the launch traced here: 13.6 us
  Pallas kernels  12.9 us (94%)
  local copies, waits for them, and re-layouts  0.66 us (5%)
    pallas_call x1, Pallas kernels, on_device(): pl.pallas_call(functools.partial(kernel, n_gx, n_gy), out_shape=jax.Shape...  12.9 us
    unnamed x1, local copies, waits for them, and re-layouts  0.66 us

profile of v8, /device:TPU:1, one launch (start us, length us, event | category | flops | bytes accessed | tf_op | source)
XLA Modules:
  0.0 13.6 jit_solution(10810716104087574200)
XLA Ops:
  0.0 12.9 %shard_map.46 = f32[4,32,256]{2,1,0:T(8,128)S(1)} custom-call(s32[1,2]{1,0:T(1,128)} %owners_in.1, f32[1,64]{1,0:T(1,128)} %bitcast.1, f32[4,32,256]{2,1,0:T(8,128)} %source_ref.1, s32[4,32,256]{2,1,0:T(8,128)} %region_ref.1), custom_call_target="tpu_custom_call" | custom-call | tf_op jit(solution)/shard_map/pallas_call | solution.py:559
  12.9 0.7 %copy.6 = f32[4,32,256]{2,1,0:T(8,128)} copy(f32[4,32,256]{2,1,0:T(8,128)S(1)} %shard_map.46) | data formatting | bytes 262144

commit v9 on v7

--- a/solution.py
+++ b/solution.py
@@ -45,7 +45,7 @@
         return (x >= 0) & (x < n_gx) & (y >= 0) & (y < n_gy)
 
     near_slabs = [
-        (dx, off) for dx in (-1, 1, 0) for off in reversed(range(n_gy)) if (dx, off) != (0, 0)
+        (dx, off) for off in reversed(range(n_gy)) for dx in (-1, 1, 0) if (dx, off) != (0, 0)
     ]
 
     nowhere = table_ref.shape[1]
@@ -122,7 +122,7 @@
             src_ref=shipped.at[2 + side],
             dst_ref=shipped.at[side],
             send_sem=send_sem.at[0],
-            recv_sem=recv_sem.at[2 * SOURCE + 1],
+            recv_sem=recv_sem.at[8],
             device_id=(gx + dx, gy),
             device_id_type=MESH,
         )
@@ -172,7 +172,7 @@
 
     def beside(kind, b):
         n = BESIDE[kind] * ny + b * CORNER[kind][0] * CORNER[kind][1]
-        return n + {REGION: 2 * EDGE, SOURCE: 2 * EDGE + ny, ITERATE: 0}[kind]
+        return n + (0 if kind == ITERATE else 2 * EDGE)
 
     def receive(kind, inner):
         def act(a, b):
@@ -187,7 +187,7 @@
         return (a * n_gy + n_gy - 1) * cx * cy * cz // nz
 
     def finish(a, b):
-        beside_x = a * sum(beside(kind, b) for kind in range(3))
+        beside_x = a * (sum(beside(kind, b) for kind in range(3)) + ny)
         wait(of_rows(3 * nx * b * HALF + beside_x), send_sem.at[0])
         wait(of_rows(2 * group_rows(a) + 8 * a * cz // nz), send_sem.at[1])
 
@@ -397,13 +397,19 @@
     second_sweep(range(first + 1, last - 1))
     with jax.named_scope("wait_source_planes"):
         receive(SOURCE, False)
-    first_sweep((first - 2, first - 1, last, last + 1))
-    second_sweep((first - 1, first, last - 1, last))
-    flux = {i: cond[i] * smooth[i] for i in smooth}
-    pairs = []
-    for i in range(cx):
-        j = first + 2 * i
-        pairs.append(defect(j, smooth, flux, ny) + defect(j + 1, smooth, flux, ny))
+    first_sweep((first - 1, last))
+    second_sweep((first, last - 1))
+    carried = {i: cond[i] * smooth[i] for i in range(first, last)}
+    left = {i: defect(i, smooth, carried, ny) for i in range(first + 1, last - 1)}
+    with jax.named_scope("wait_shipped"):
+        by_neighbours(lambda a, b: wait(of_rows(a * ny), recv_sem.at[8]))
+    first_sweep((first - 2, last + 1))
+    second_sweep((first - 1, last))
+    for i in (first - 1, last):
+        carried[i] = cond[i] * smooth[i]
+    for i in (first, last - 1):
+        left[i] = defect(i, smooth, carried, ny)
+    pairs = [left[first + 2 * i] + left[first + 2 * i + 1] for i in range(cx)]
     coarsen(pairs, 1)
     with jax.named_scope("start_coarse_res"):
         gather_start(1)
@@ -564,7 +570,7 @@
             pltpu.VMEM((cx + 2, all_y + 16, cz), f32),
             pltpu.VMEM((cx + 2, 2, ny + 8, cz), f32),
             pltpu.SemaphoreType.DMA((2,)),
-            pltpu.SemaphoreType.DMA((8,)),
+            pltpu.SemaphoreType.DMA((9,)),
             pltpu.SemaphoreType.DMA((4,)),
             pltpu.SemaphoreType.REGULAR,
             pltpu.SemaphoreType.REGULAR,

time: 13.7 us -> 13.7 us (level)
  no operation moved by 1% of the time
where the time goes in v9:
time: 13.7 us; the launch traced here: 13.6 us
  Pallas kernels  12.9 us (94%)
  local copies, waits for them, and re-layouts  0.66 us (5%)
    pallas_call x1, Pallas kernels, on_device(): pl.pallas_call(functools.partial(kernel, n_gx, n_gy), out_shape=jax.Shape...  12.9 us
    unnamed x1, local copies, waits for them, and re-layouts  0.66 us

profile of v9, /device:TPU:9, one launch (start us, length us, event | category | flops | bytes accessed | tf_op | source)
XLA Modules:
  0.0 13.6 jit_solution(6676791114686005567)
XLA Ops:
  0.0 12.9 %shard_map.46 = f32[4,32,256]{2,1,0:T(8,128)S(1)} custom-call(s32[1,2]{1,0:T(1,128)} %owners_in.1, f32[1,64]{1,0:T(1,128)} %bitcast.1, f32[4,32,256]{2,1,0:T(8,128)} %source_ref.1, s32[4,32,256]{2,1,0:T(8,128)} %region_ref.1), custom_call_target="tpu_custom_call" | custom-call | tf_op jit(solution)/shard_map/pallas_call | solution.py:556
  12.9 0.7 %copy.6 = f32[4,32,256]{2,1,0:T(8,128)} copy(f32[4,32,256]{2,1,0:T(8,128)S(1)} %shard_map.46) | data formatting | bytes 262144

commit v10 on v9

--- a/solution.py
+++ b/solution.py
@@ -102,9 +102,9 @@
         return pltpu.make_async_remote_copy(
             src_ref=fields[kind].at[pl.ds(first + plane, w), pl.ds(row, high)],
             dst_ref=fields[kind].at[pl.ds(land, w), pl.ds(to, high)],
-            send_sem=send_sem.at[0],
-            recv_sem=recv_sem.at[
-                5 if kind == REGION and dx * dy else 2 * kind + abs(dx) * (kind != ITERATE)
+            send_sem=send_sem,
+            recv_sem=in_sem.at[0] if kind == ITERATE else recv_sem.at[
+                4 if kind == REGION and dx * dy else 2 * kind + abs(dx)
             ],
             device_id=(gx + dx, gy + dy),
             device_id_type=MESH,
@@ -121,8 +121,8 @@
         return pltpu.make_async_remote_copy(
             src_ref=shipped.at[2 + side],
             dst_ref=shipped.at[side],
-            send_sem=send_sem.at[0],
-            recv_sem=recv_sem.at[8],
+            send_sem=send_sem,
+            recv_sem=recv_sem.at[5],
             device_id=(gx + dx, gy),
             device_id_type=MESH,
         )
@@ -179,7 +179,7 @@
             n = nx * b * HALF if inner else a * beside(kind, 0 if kind == REGION else b)
             if kind == ITERATE:
                 n += nx * b * HALF
-            wait(of_rows(n), recv_sem.at[2 * kind + (not inner and kind != ITERATE)])
+            wait(of_rows(n), in_sem.at[0] if kind == ITERATE else recv_sem.at[2 * kind + (not inner)])
 
         by_neighbours(act)
 
@@ -188,8 +188,8 @@
 
     def finish(a, b):
         beside_x = a * (sum(beside(kind, b) for kind in range(3)) + ny)
-        wait(of_rows(3 * nx * b * HALF + beside_x), send_sem.at[0])
-        wait(of_rows(2 * group_rows(a) + 8 * a * cz // nz), send_sem.at[1])
+        blocks = 2 * group_rows(a) + 8 * a * cz // nz
+        wait(of_rows(3 * nx * b * HALF + beside_x + blocks), send_sem)
 
     def gather(kind, dx, off):
         at = pl.ds(pl.multiple_of(all_y + gy * cy, 8), cy)
@@ -197,8 +197,8 @@
         return pltpu.make_async_remote_copy(
             src_ref=group.at[kind, :, at],
             dst_ref=group.at[kind, :, to],
-            send_sem=send_sem.at[1],
-            recv_sem=recv_sem.at[6 + kind],
+            send_sem=send_sem,
+            recv_sem=in_sem.at[1] if kind else recv_sem.at[6],
             device_id=(gx + dx, lax.rem(gy + off, n_gy)),
             device_id_type=MESH,
         )
@@ -207,7 +207,7 @@
         return pltpu.make_async_remote_copy(
             src_ref=holders.at[1],
             dst_ref=holders.at[1 - dx],
-            send_sem=send_sem.at[1],
+            send_sem=send_sem,
             recv_sem=recv_sem.at[6],
             device_id=(gx + dx, gy),
             device_id_type=MESH,
@@ -222,7 +222,7 @@
     def gather_wait(kind):
         told = 0 if kind else 8 * cz // nz
         by_neighbours(lambda a, b: wait(
-            of_rows(group_rows(a) + a * told), recv_sem.at[6 + kind]
+            of_rows(group_rows(a) + a * told), in_sem.at[1] if kind else recv_sem.at[6]
         ))
 
     for dy in (-1, 1):
@@ -364,7 +364,7 @@
     look_up(edges, range(0, ny, 8))
     with jax.named_scope("wait_region_corners"):
         by_neighbours(lambda a, b: wait(
-            of_rows(a * b * CORNER[REGION][0] * CORNER[REGION][1]), recv_sem.at[5]
+            of_rows(a * b * CORNER[REGION][0] * CORNER[REGION][1]), recv_sem.at[4]
         ))
     look_up(edges, (ny,))
     weigh([first - 2, first - 1, first, last - 1, last, last + 1])
@@ -402,7 +402,7 @@
     carried = {i: cond[i] * smooth[i] for i in range(first, last)}
     left = {i: defect(i, smooth, carried, ny) for i in range(first + 1, last - 1)}
     with jax.named_scope("wait_shipped"):
-        by_neighbours(lambda a, b: wait(of_rows(a * ny), recv_sem.at[8]))
+        by_neighbours(lambda a, b: wait(of_rows(a * ny), recv_sem.at[5]))
     first_sweep((first - 2, last + 1))
     second_sweep((first - 1, last))
     for i in (first - 1, last):
@@ -562,15 +562,15 @@
             pltpu.SMEM((1, n_gy), jnp.int32),
             pltpu.VMEM((1, permeability.shape[0]), f32),
             pltpu.VMEM((planes, ny + 8, nz), jnp.int32),
-            pltpu.VMEM((8 * planes, ny + 8, nz), f32),
+            pltpu.VMEM((15 * planes, ny + 8, nz), f32),
             pltpu.VMEM((4, ny, nz), f32),
             pltpu.VMEM((2, cx, 3 * all_y, cz), f32),
             pltpu.VMEM((3, 8, cz), f32),
             pltpu.VMEM((cx, ny, cz), f32),
             pltpu.VMEM((cx + 2, all_y + 16, cz), f32),
             pltpu.VMEM((cx + 2, 2, ny + 8, cz), f32),
-            pltpu.SemaphoreType.DMA((2,)),
-            pltpu.SemaphoreType.DMA((9,)),
+            pltpu.SemaphoreType.DMA,
+            pltpu.SemaphoreType.DMA((7,)),
             pltpu.SemaphoreType.DMA((4,)),
             pltpu.SemaphoreType.REGULAR,
             pltpu.SemaphoreType.REGULAR,

time: 13.7 us -> 13.7 us (level)
  no operation moved by 1% of the time
where the time goes in v10:
time: 13.7 us; the launch traced here: 13.6 us
  Pallas kernels  12.9 us (94%)
  local copies, waits for them, and re-layouts  0.66 us (5%)
    pallas_call x1, Pallas kernels, on_device(): pl.pallas_call(functools.partial(kernel, n_gx, n_gy), out_shape=jax.Shape...  12.9 us
    unnamed x1, local copies, waits for them, and re-layouts  0.66 us

profile of v10, /device:TPU:9, one launch (start us, length us, event | category | flops | bytes accessed | tf_op | source)
XLA Modules:
  0.0 13.6 jit_solution(13738557483951113790)
XLA Ops:
  0.0 12.9 %shard_map.46 = f32[4,32,256]{2,1,0:T(8,128)S(1)} custom-call(s32[1,2]{1,0:T(1,128)} %owners_in.1, f32[1,64]{1,0:T(1,128)} %bitcast.1, f32[4,32,256]{2,1,0:T(8,128)} %source_ref.1, s32[4,32,256]{2,1,0:T(8,128)} %region_ref.1), custom_call_target="tpu_custom_call" | custom-call | tf_op jit(solution)/shard_map/pallas_call | solution.py:556
  12.9 0.7 %copy.6 = f32[4,32,256]{2,1,0:T(8,128)} copy(f32[4,32,256]{2,1,0:T(8,128)S(1)} %shard_map.46) | data formatting | bytes 262144
